TPU v7x, 512 devices: a whole 4x4x16 slice. The times are simulated.
512 devices in a mesh: scene: 4 (over x), dom: 128 (over y, z, core).
Axes of the slice: x: 4, y: 4, z: 16, core: 2. Of those that a mesh axis runs over, the one named last changes fastest.
Arguments:
- features: bfloat16 [1024, 8, 8, 512], P(('scene', 'dom')), parts along dimension 0, may hold values from -5 to 5
- weight_first: bfloat16 [3, 3, 3, 64, 64], replicated, may hold values from -0.15625 to 0.15625
- weight_second: bfloat16 [3, 3, 3, 64, 64], replicated, may hold values from -0.15625 to 0.15625
- neighbours: int32 [1024, 26], P(('scene', 'dom')), parts along dimension 0, may hold values from -1 to 255, as said below
- active: int32 [1024], P(('scene', 'dom')), parts along dimension 0, may hold values from 0 to 1, as said below
- cotangent: bfloat16 [1024, 8, 8, 512], P(('scene', 'dom')), parts along dimension 0, may hold values from -5 to 5
Outputs:
- output: bfloat16 [1024, 8, 8, 512], P(('scene', 'dom')), parts along dimension 0
- grad_features: bfloat16 [1024, 8, 8, 512], P(('scene', 'dom')), parts along dimension 0
- filter_grad_first: float32 [12, 3, 3, 64, 64], P('scene'), parts along dimension 0
- filter_grad_second: float32 [12, 3, 3, 64, 64], P('scene'), parts along dimension 0
There are 4 independent parts, one for each index of `scene`. A program takes and returns all parts, laid end to end along the dimension named above; an argument that names none is the same for every part. Nothing has to cross between parts.
Inputs may be any that keep to these rules, and one draw needn't show every extreme that they name: `neighbours`: offsets (dx, dy, dz) run over the finite set (-1, 0, 1) cubed without (0, 0, 0), in lexicographic order with dx slowest. Entry k of row b is the id of the active brick whose voxels continue those of brick b at offset k, or -1; rows of inactive bricks are all -1. The relation is symmetric: b lists c at an offset exactly when c lists b at the opposite one. A brick listed at dx = 0 has the same id // 2 as b; at dx = -1 or +1 its id // 2 is one lower or one higher. Some index of dom has all of its 2 slots active.
All inputs are finite; a program needn't handle non-finite values.
Results may differ from a plain program's by a relative error of at most 0.0035.
Values may be sent and summed in bfloat16 or wider, within the bound.
A program may use at most 64 MiB of HBM per device.

v0:
```python
import math

import jax
import jax.numpy as jnp
from jax import lax
from jax.sharding import PartitionSpec as P

C = 64
E = 8


def with_halo(block, sides, width):
    for axis, dim in sides:
        count = lax.axis_size(axis)
        forward = [(i, i + 1) for i in range(count - 1)]
        backward = [(target, source) for source, target in forward]
        low = lax.ppermute(
            lax.slice_in_dim(block, block.shape[dim] - width, None, axis=dim), axis, forward
        )
        high = lax.ppermute(lax.slice_in_dim(block, 0, width, axis=dim), axis, backward)
        block = jnp.concatenate([low, block, high], axis=dim)
    return block


def directions():
    offsets_all = []
    for step_x in (-1, 0, 1):
        for step_y in (-1, 0, 1):
            for step_z in (-1, 0, 1):
                if (step_x, step_y, step_z) != (0, 0, 0):
                    offsets_all.append((step_x, step_y, step_z))
    return offsets_all


def source_range(offset, length):
    if offset < 0:
        return (length - 1, length)
    if offset > 0:
        return (0, 1)
    return (0, length)


def join_blocks(blocks):
    planes = []
    for step_x in (-1, 0, 1):
        row_list = []
        for step_y in (-1, 0, 1):
            row_list.append(
                jnp.concatenate([blocks[step_x, step_y, step_z] for step_z in (-1, 0, 1)], axis=3)
            )
        planes.append(jnp.concatenate(row_list, axis=2))
    return jnp.concatenate(planes, axis=1)


def with_blank(values):
    return jnp.concatenate([values, jnp.zeros((1,) + values.shape[1:], values.dtype)], axis=0)


def layer_pair(values):
    slot_count, length = (values.shape[0], values.shape[1])
    stacked = jnp.stack([values[:, 0], values[:, length - 1]])
    return stacked.reshape(2, slot_count, length, length * values.shape[4])


def unpack_layers(around, like):
    layer_shape = (like.shape[0], 1) + like.shape[2:]
    return (around[0].reshape(layer_shape), around[3].reshape(layer_shape))


def pad_from(center, around, lookup):
    lower, upper = unpack_layers(around, center)
    sources = {-1: with_blank(lower), 0: with_blank(center), 1: with_blank(upper)}
    blocks = {(0, 0, 0): center}
    for number, offset in enumerate(directions()):
        range_x = source_range(0, E) if offset[0] == 0 else (0, 1)
        range_y = source_range(offset[1], E)
        range_z = source_range(offset[2], E)
        portion = sources[offset[0]][
            :, range_x[0] : range_x[1], range_y[0] : range_y[1], range_z[0] : range_z[1]
        ]
        blocks[offset] = jnp.take(portion, lookup[:, number], axis=0)
    return join_blocks(blocks)


def convolve(padded, kernel):
    return lax.conv_general_dilated(
        padded,
        kernel,
        (1, 1, 1),
        "VALID",
        dimension_numbers=("NDHWC", "DHWIO", "NDHWC"),
        preferred_element_type=jnp.float32,
    )


def flip_kernel(kernel):
    return jnp.flip(kernel, (0, 1, 2)).transpose(0, 1, 2, 4, 3)


def weight_grad(padded, grads):
    tap_list = []
    for shift_x in range(3):
        for shift_y in range(3):
            for shift_z in range(3):
                window = padded[
                    :, shift_x : shift_x + E, shift_y : shift_y + E, shift_z : shift_z + E
                ]
                tap_list.append(
                    jnp.einsum("nxyzi,nxyzo->io", window, grads, preferred_element_type=jnp.float32)
                )
    return jnp.stack(tap_list).reshape(3, 3, 3, C, C)


def silu_slope(inputs):
    sigmoid_val = jax.nn.sigmoid(inputs)
    return sigmoid_val * (1.0 + inputs * (1.0 - sigmoid_val))


def on_device(features, weight_first, weight_second, neighbours, active, cotangent):
    slot_count = features.shape[0]
    bricks = features.reshape(slot_count, E, E, E, C)
    grad_given = cotangent.reshape(slot_count, E, E, E, C)
    lookup = jnp.where(neighbours < 0, slot_count, neighbours % slot_count)
    alive_mask = active.astype(jnp.float32).reshape(slot_count, 1, 1, 1, 1)
    around_in = with_halo(layer_pair(bricks), (("dom", 0),), 1)
    padded_in = pad_from(bricks, around_in, lookup)
    hidden_pre = convolve(padded_in, weight_first)
    middle = (alive_mask * jax.nn.silu(hidden_pre)).astype(jnp.bfloat16)
    around_mid = with_halo(layer_pair(middle), (("dom", 0),), 1)
    padded_mid = pad_from(middle, around_mid, lookup)
    block_out = convolve(padded_mid, weight_second)
    output = (bricks.astype(jnp.float32) + block_out).astype(jnp.bfloat16)
    grad_out = (alive_mask * grad_given.astype(jnp.float32)).astype(jnp.bfloat16)
    filter_second = weight_grad(padded_mid, grad_out)
    around_go = with_halo(layer_pair(grad_out), (("dom", 0),), 1)
    grad_middle = convolve(pad_from(grad_out, around_go, lookup), flip_kernel(weight_second))
    grad_hidden = (grad_middle * silu_slope(hidden_pre)).astype(jnp.bfloat16)
    filter_first = weight_grad(padded_in, grad_hidden)
    around_gh = with_halo(layer_pair(grad_hidden), (("dom", 0),), 1)
    grad_input = convolve(pad_from(grad_hidden, around_gh, lookup), flip_kernel(weight_first))
    grad_features = (alive_mask * (grad_given.astype(jnp.float32) + grad_input)).astype(
        jnp.bfloat16
    )
    grad_scale = 1.0 / math.sqrt(slot_count * lax.axis_size("dom") * E**3)
    filter_first, filter_second = lax.psum((filter_first, filter_second), "dom")
    first_out = filter_first * grad_scale
    second_out = filter_second * grad_scale
    return (
        output.reshape(features.shape),
        grad_features.reshape(features.shape),
        first_out,
        second_out,
    )


def solution(mesh):
    return jax.shard_map(
        on_device,
        mesh=mesh,
        in_specs=(
            P(("scene", "dom"), None, None, None),
            P(),
            P(),
            P(("scene", "dom"), None),
            P(("scene", "dom")),
            P(("scene", "dom"), None, None, None),
        ),
        out_specs=(
            P(("scene", "dom"), None, None, None),
            P(("scene", "dom"), None, None, None),
            P("scene", None, None, None, None),
            P("scene", None, None, None, None),
        ),
        check_vma=False,
    )
```

profile of v0, /device:TPU:1, one launch (start us, length us, event | category | flops | bytes accessed | tf_op | source)
XLA Modules:
  0.0 604.1 jit_solution(14665672001398796384)
XLA Ops:
  7.2 1.1 reshape.161
  9.9 8.8 %collective-permute-start.5 = (bf16[1,2,8,512]{3,2,1,0:T(8,128)(2,1)S(1)}, bf16[1,2,8,512]{3,2,1,0:T(8,128)(2,1)S(1)}, u32[]{:S(2)}, u32[]{:S(2)}) collective-permute-start(bf16[1,2,8,512]{3,2,1,0:T(8,128)(2,1)S(1)} %slice.809), channel_id=1, source_target_pairs={{1,0},{2,1},{3,2},{4,3},{5,4},{6,5},{7,6},{8,7},{9,8},{10,9},{11,1... | collective-permute-start | bytes 49160 | tf_op jit(solution)/shard_map/ppermute | solution.py:20
  18.8 1.9 collective-permute-start.4
  21.0 2.4 collective-permute-start.1
  23.5 3.2 collective-permute-start
  45.3 1.4 maximum_maximum_fusion.12
  46.7 1.5 fusion.205
  48.2 1.5 fusion.204
  77.6 1.2 maximum_maximum_fusion.1
  78.8 5.5 fusion.60
  84.5 2.7 fusion.64
  93.0 2.8 maximum_maximum_fusion.9
  95.9 6.5 %maximum_maximum_fusion.10 = bf16[2,9,10,10,64]{4,0,3,2,1:T(2,128)(2,1)S(1)} fusion(bf16[2,1,1,1,64]{4,0,3,2,1:T(2,128)(2,1)S(1)} %copy-done.117, bf16[2,1,1,8,64]{4,0,3,2,1:T(2,128)(2,1)S(1)} %broadcast_select_fusion.36, bf16[2,1,1,1,64]{4,0,3,2,1:T(2,128)(2,1)S(1)} %copy-done.119, bf16[2,1,8,1,64]{4,0,3,2,1:T(2,128)(2,1)S(1)} %broadcast_select_fusion.37, ...), kind=kLoop, calls=%fused_computation.270 | loop fusion | flops 1958400 | bytes 460800 | tf_op jit(solution)/shard_map/concatenate | solution.py:52
  102.6 1.5 slice.837
  104.1 1.9 collective-permute-start.7
  106.0 1.4 slice.781
  107.4 2.1 collective-permute-start.3
  110.2 1.3 gather_fusion.94
  112.2 1.3 gather_fusion.42
  113.5 1.5 gather_fusion.93
  114.9 1.5 gather_fusion.41
  117.1 1.3 gather_fusion.92
  119.1 1.3 gather_fusion.40
  120.4 0.9 copy.912
  122.0 0.9 copy.914
  131.2 3.6 collective-permute-start.6
  135.6 2.4 collective-permute-start.2
  138.0 2.6 fusion.203
  140.6 0.9 fusion.53
  148.3 0.9 fusion.44
  149.3 0.9 fusion.43
  150.2 0.9 fusion.42
  151.1 0.9 fusion.41
  153.0 2.3 fusion.202
  156.9 1.0 fusion.39
  157.9 0.9 fusion.38
  158.8 0.9 fusion.37
  159.8 0.9 fusion.36
  167.5 0.9 fusion.27
  168.3 1.8 maximum_maximum_fusion.6
  176.9 1.2 gather_fusion.103
  178.0 1.2 gather_fusion.51
  179.3 1.3 gather_fusion.102
  180.6 1.3 gather_fusion.50
  181.8 1.3 gather_fusion.101
  183.1 1.2 gather_fusion.49
  184.3 1.3 gather_fusion.100
  185.6 1.3 gather_fusion.48
  189.7 1.4 gather_fusion.97
  191.1 1.4 gather_fusion.45
  193.8 1.4 gather_fusion.95
  195.2 1.3 gather_fusion.43
  196.5 1.4 gather_fusion.86
  197.9 1.4 gather_fusion.34
  200.6 1.4 gather_fusion.84
  202.0 1.4 gather_fusion.32
  226.8 3.4 fusion.62
  231.2 6.5 %fusion.58 = f32[2,8,8,8,64]{4,0,3,2,1:T(2,128)} fusion(bf16[3,3,3,64,64]{4,3,2,1,0:T(8,128)(2,1)S(1)} %copy-done.131, bf16[2,10,10,10,64]{4,3,2,1,0:T(8,128)(2,1)S(1)} %maximum_maximum_fusion.2), kind=kOutput, calls=%fused_computation.262 | convolution fusion | flops 226492416 | bytes 739328 | tf_op jit(solution)/shard_map/conv_general_dilated | solution.py:86
  245.5 0.9 copy-done.2
  246.9 0.9 reshape.157
  248.0 0.9 reshape.158
  248.9 344.8 %all-reduce.15.cloned.1.call-done = (f32[3,3,3,64,64]{4,3,2,1,0:T(8,128)}, f32[3,3,3,64,64]{4,3,2,1,0:T(8,128)}) async-done(((f32[3,3,3,64,64]{4,3,2,1,0:T(8,128)}, f32[3,3,3,64,64]{4,3,2,1,0:T(8,128)}), (f32[3,3,3,64,64]{4,3,2,1,0:T(8,128)}, f32[3,3,3,64,64]{4,3,2,1,0:T(8,128)})) %all-reduce.15.cloned.1.call-update) | async-done | bytes 884752 | tf_op jit(solution)/shard_map/psum | solution.py:145
  593.8 2.3 broadcast_multiply_fusion.1
  596.0 1.0 broadcast_multiply_fusion
  (674 shorter events, 126.8 us)
Async XLA Ops:
  7.2 71.6 %copy-start = (bf16[3,3,3,64,64]{4,3,2,1,0:T(8,128)(2,1)S(1)}, bf16[3,3,3,64,64]{4,3,2,1,0:T(8,128)(2,1)}, u32[]{:S(2)}) copy-start(bf16[3,3,3,64,64]{4,3,2,1,0:T(8,128)(2,1)} %param.22) | copy-start | bytes 663556
  7.2 586.6 %all-reduce.15.cloned.1.call-start = ((), (), s32[]{:S(2)}) async-start(), calls=%async_computation | async-start | bytes 3538944 | tf_op jit(solution)/shard_map/psum | solution.py:145
  8.4 18.3 %copy-start.116 = (s32[2,26]{1,0:T(2,128)S(1)}, s32[2,26]{1,0:T(2,128)}, u32[]{:S(2)}) copy-start(s32[2,26]{1,0:T(2,128)} %param.23) | copy-start | bytes 628
  9.9 41.3 %collective-permute-start.5 = (bf16[1,2,8,512]{3,2,1,0:T(8,128)(2,1)S(1)}, bf16[1,2,8,512]{3,2,1,0:T(8,128)(2,1)S(1)}, u32[]{:S(2)}, u32[]{:S(2)}) collective-permute-start(bf16[1,2,8,512]{3,2,1,0:T(8,128)(2,1)S(1)} %slice.809), channel_id=1, source_target_pairs={{1,0},{2,1},{3,2},{4,3},{5,4},{6,5},{7,6},{8,7},{9,8},{10,9},{11,1... | collective-permute-start | bytes 49160 | tf_op jit(solution)/shard_map/ppermute | solution.py:20
  18.8 32.6 %collective-permute-start.4 = (bf16[1,2,8,512]{3,2,1,0:T(8,128)(2,1)S(1)}, bf16[1,2,8,512]{3,2,1,0:T(8,128)(2,1)S(1)}, u32[]{:S(2)}, u32[]{:S(2)}) collective-permute-start(bf16[1,2,8,512]{3,2,1,0:T(8,128)(2,1)S(1)} %slice.791), channel_id=1, source_target_pairs={{0,1},{1,2},{2,3},{3,4},{4,5},{5,6},{6,7},{7,8},{8,9},{9,10},{10,1... | collective-permute-start | bytes 49160 | tf_op jit(solution)/shard_map/ppermute | solution.py:17
  21.0 30.7 %collective-permute-start.1 = (bf16[1,2,8,512]{3,2,1,0:T(8,128)(2,1)S(1)}, bf16[1,2,8,512]{3,2,1,0:T(8,128)(2,1)S(1)}, u32[]{:S(2)}, u32[]{:S(2)}) collective-permute-start(bf16[1,2,8,512]{3,2,1,0:T(8,128)(2,1)S(1)} %slice.744), channel_id=1, source_target_pairs={{1,0},{2,1},{3,2},{4,3},{5,4},{6,5},{7,6},{8,7},{9,8},{10,9},{11,1... | collective-permute-start | bytes 49160 | tf_op jit(solution)/shard_map/ppermute | solution.py:20
  23.5 28.5 %collective-permute-start = (bf16[1,2,8,512]{3,2,1,0:T(8,128)(2,1)S(1)}, bf16[1,2,8,512]{3,2,1,0:T(8,128)(2,1)S(1)}, u32[]{:S(2)}, u32[]{:S(2)}) collective-permute-start(bf16[1,2,8,512]{3,2,1,0:T(8,128)(2,1)S(1)} %slice.709), channel_id=1, source_target_pairs={{0,1},{1,2},{2,3},{3,4},{4,5},{5,6},{6,7},{7,8},{8,9},{9,10},{10,1... | collective-permute-start | bytes 49160 | tf_op jit(solution)/shard_map/ppermute | solution.py:17
  28.3 27.1 %copy-start.88 = (pred[2]{0:T(512)(128)(4,1)}, pred[2]{0:T(512)(128)(4,1)S(1)}, u32[]{:S(2)}) copy-start(pred[2]{0:T(512)(128)(4,1)S(1)} %get-tuple-element.245) | copy-start | bytes 10
  28.9 29.7 %copy-start.87 = (pred[2]{0:T(512)(128)(4,1)}, pred[2]{0:T(512)(128)(4,1)S(1)}, u32[]{:S(2)}) copy-start(pred[2]{0:T(512)(128)(4,1)S(1)} %get-tuple-element.247) | copy-start | bytes 10
  34.2 18.8 %copy-start.62 = (s32[1024]{0:T(1024)}, s32[1024]{0:T(1024)S(1)}, u32[]{:S(2)}) copy-start(s32[1024]{0:T(1024)S(1)} %pad_clamp_fusion) | copy-start | bytes 12292
  34.2 20.6 %copy-start.61 = (s32[1024]{0:T(1024)}, s32[1024]{0:T(1024)S(1)}, u32[]{:S(2)}) copy-start(s32[1024]{0:T(1024)S(1)} %pad_clamp_fusion.1) | copy-start | bytes 12292
  34.2 22.5 %copy-start.60 = (s32[1024]{0:T(1024)}, s32[1024]{0:T(1024)S(1)}, u32[]{:S(2)}) copy-start(s32[1024]{0:T(1024)S(1)} %pad_clamp_fusion.2) | copy-start | bytes 12292
  34.3 23.7 %copy-start.59 = (s32[1024]{0:T(1024)}, s32[1024]{0:T(1024)S(1)}, u32[]{:S(2)}) copy-start(s32[1024]{0:T(1024)S(1)} %pad_clamp_fusion.3) | copy-start | bytes 12292
  34.3 25.6 %copy-start.49 = (s32[1024]{0:T(1024)}, s32[1024]{0:T(1024)S(1)}, u32[]{:S(2)}) copy-start(s32[1024]{0:T(1024)S(1)} %pad_clamp_fusion.4) | copy-start | bytes 12292
  34.3 27.0 %copy-start.58 = (s32[1024]{0:T(1024)}, s32[1024]{0:T(1024)S(1)}, u32[]{:S(2)}) copy-start(s32[1024]{0:T(1024)S(1)} %pad_clamp_fusion.5) | copy-start | bytes 12292
  34.3 28.2 %copy-start.57 = (s32[1024]{0:T(1024)}, s32[1024]{0:T(1024)S(1)}, u32[]{:S(2)}) copy-start(s32[1024]{0:T(1024)S(1)} %pad_clamp_fusion.6) | copy-start | bytes 12292
  34.4 29.5 %copy-start.56 = (s32[1024]{0:T(1024)}, s32[1024]{0:T(1024)S(1)}, u32[]{:S(2)}) copy-start(s32[1024]{0:T(1024)S(1)} %pad_clamp_fusion.7) | copy-start | bytes 12292
  34.4 30.8 %copy-start.55 = (s32[1024]{0:T(1024)}, s32[1024]{0:T(1024)S(1)}, u32[]{:S(2)}) copy-start(s32[1024]{0:T(1024)S(1)} %pad_clamp_fusion.8) | copy-start | bytes 12292
  49.7 16.8 %copy-start.70 = (s32[1024]{0:T(1024)}, s32[1024]{0:T(1024)S(1)}, u32[]{:S(2)}) copy-start(s32[1024]{0:T(1024)S(1)} %get-tuple-element.261) | copy-start | bytes 12292
  49.7 18.1 %copy-start.69 = (s32[1024]{0:T(1024)}, s32[1024]{0:T(1024)S(1)}, u32[]{:S(2)}) copy-start(s32[1024]{0:T(1024)S(1)} %get-tuple-element.262) | copy-start | bytes 12292
  49.7 19.3 %copy-start.68 = (s32[1024]{0:T(1024)}, s32[1024]{0:T(1024)S(1)}, u32[]{:S(2)}) copy-start(s32[1024]{0:T(1024)S(1)} %get-tuple-element.263) | copy-start | bytes 12292
  49.7 20.6 %copy-start.67 = (s32[1024]{0:T(1024)}, s32[1024]{0:T(1024)S(1)}, u32[]{:S(2)}) copy-start(s32[1024]{0:T(1024)S(1)} %get-tuple-element.264) | copy-start | bytes 12292
  49.8 21.9 %copy-start.50 = (s32[1024]{0:T(1024)}, s32[1024]{0:T(1024)S(1)}, u32[]{:S(2)}) copy-start(s32[1024]{0:T(1024)S(1)} %get-tuple-element.265) | copy-start | bytes 12292
  49.8 23.2 %copy-start.66 = (s32[1024]{0:T(1024)}, s32[1024]{0:T(1024)S(1)}, u32[]{:S(2)}) copy-start(s32[1024]{0:T(1024)S(1)} %get-tuple-element.266) | copy-start | bytes 12292
  49.8 24.5 %copy-start.65 = (s32[1024]{0:T(1024)}, s32[1024]{0:T(1024)S(1)}, u32[]{:S(2)}) copy-start(s32[1024]{0:T(1024)S(1)} %get-tuple-element.267) | copy-start | bytes 12292
  49.8 25.8 %copy-start.64 = (s32[1024]{0:T(1024)}, s32[1024]{0:T(1024)S(1)}, u32[]{:S(2)}) copy-start(s32[1024]{0:T(1024)S(1)} %get-tuple-element.268) | copy-start | bytes 12292
  49.8 27.1 %copy-start.63 = (s32[1024]{0:T(1024)}, s32[1024]{0:T(1024)S(1)}, u32[]{:S(2)}) copy-start(s32[1024]{0:T(1024)S(1)} %pad_clamp_fusion.25) | copy-start | bytes 12292
  51.7 15.3 %copy-start.115 = (pred[2]{0:T(512)(128)(4,1)S(1)}, pred[2]{0:T(512)(128)(4,1)}, u32[]{:S(2)}) copy-start(pred[2]{0:T(512)(128)(4,1)} %compare_and_fusion.18) | copy-start | bytes 10
  51.8 16.5 %copy-start.91 = (pred[2]{0:T(512)(128)(4,1)S(1)}, pred[2]{0:T(512)(128)(4,1)}, u32[]{:S(2)}) copy-start(pred[2]{0:T(512)(128)(4,1)} %get-tuple-element.275) | copy-start | bytes 10
  51.8 17.8 %copy-start.107 = (pred[2]{0:T(512)(128)(4,1)S(1)}, pred[2]{0:T(512)(128)(4,1)}, u32[]{:S(2)}) copy-start(pred[2]{0:T(512)(128)(4,1)} %get-tuple-element.276) | copy-start | bytes 10
  51.9 19.0 %copy-start.90 = (pred[2]{0:T(512)(128)(4,1)S(1)}, pred[2]{0:T(512)(128)(4,1)}, u32[]{:S(2)}) copy-start(pred[2]{0:T(512)(128)(4,1)} %get-tuple-element.277) | copy-start | bytes 10
  52.1 20.1 %copy-start.76 = (pred[2]{0:T(512)(128)(4,1)S(1)}, pred[2]{0:T(512)(128)(4,1)}, u32[]{:S(2)}) copy-start(pred[2]{0:T(512)(128)(4,1)} %get-tuple-element.278) | copy-start | bytes 10
  52.2 21.4 %copy-start.89 = (pred[2]{0:T(512)(128)(4,1)S(1)}, pred[2]{0:T(512)(128)(4,1)}, u32[]{:S(2)}) copy-start(pred[2]{0:T(512)(128)(4,1)} %get-tuple-element.279) | copy-start | bytes 10
  52.2 22.6 %copy-start.106 = (pred[2]{0:T(512)(128)(4,1)S(1)}, pred[2]{0:T(512)(128)(4,1)}, u32[]{:S(2)}) copy-start(pred[2]{0:T(512)(128)(4,1)} %get-tuple-element.280) | copy-start | bytes 10
  52.2 23.9 %copy-start.100 = (pred[2]{0:T(512)(128)(4,1)S(1)}, pred[2]{0:T(512)(128)(4,1)}, u32[]{:S(2)}) copy-start(pred[2]{0:T(512)(128)(4,1)} %compare_and_fusion.25) | copy-start | bytes 10
  52.3 25.2 %copy-start.101 = (pred[2]{0:T(512)(128)(4,1)S(1)}, pred[2]{0:T(512)(128)(4,1)}, u32[]{:S(2)}) copy-start(pred[2]{0:T(512)(128)(4,1)} %get-tuple-element.243) | copy-start | bytes 10
  57.4 26.9 %copy-start.118 = (bf16[2,1,1,1,64]{4,0,3,2,1:T(2,128)(2,1)}, bf16[2,1,1,1,64]{4,0,3,2,1:T(2,128)(2,1)S(1)}, u32[]{:S(2)}) copy-start(bf16[2,1,1,1,64]{4,0,3,2,1:T(2,128)(2,1)S(1)} %broadcast_select_fusion.73) | copy-start | bytes 772
  60.7 23.7 %copy-start.15 = (bf16[2,1,8,8,64]{4,0,3,2,1:T(2,128)(2,1)}, bf16[2,1,8,8,64]{4,0,3,2,1:T(2,128)(2,1)S(1)}, u32[]{:S(2)}) copy-start(bf16[2,1,8,8,64]{4,0,3,2,1:T(2,128)(2,1)S(1)} %broadcast_select_fusion.6) | copy-start | bytes 49156
  62.0 22.3 %copy-start.29 = (bf16[2,1,8,1,64]{4,0,3,2,1:T(2,128)(2,1)}, bf16[2,1,8,1,64]{4,0,3,2,1:T(2,128)(2,1)S(1)}, u32[]{:S(2)}) copy-start(bf16[2,1,8,1,64]{4,0,3,2,1:T(2,128)(2,1)S(1)} %broadcast_select_fusion.38) | copy-start | bytes 6148
  63.3 21.1 %copy-start.120 = (bf16[2,1,1,1,64]{4,0,3,2,1:T(2,128)(2,1)}, bf16[2,1,1,1,64]{4,0,3,2,1:T(2,128)(2,1)S(1)}, u32[]{:S(2)}) copy-start(bf16[2,1,1,1,64]{4,0,3,2,1:T(2,128)(2,1)S(1)} %broadcast_select_fusion.74) | copy-start | bytes 772
  64.6 19.8 %copy-start.31 = (bf16[2,1,1,8,64]{4,0,3,2,1:T(2,128)(2,1)}, bf16[2,1,1,8,64]{4,0,3,2,1:T(2,128)(2,1)S(1)}, u32[]{:S(2)}) copy-start(bf16[2,1,1,8,64]{4,0,3,2,1:T(2,128)(2,1)S(1)} %broadcast_select_fusion.39) | copy-start | bytes 6148
  65.9 18.5 %copy-start.122 = (bf16[2,1,1,1,64]{4,0,3,2,1:T(2,128)(2,1)}, bf16[2,1,1,1,64]{4,0,3,2,1:T(2,128)(2,1)S(1)}, u32[]{:S(2)}) copy-start(bf16[2,1,1,1,64]{4,0,3,2,1:T(2,128)(2,1)S(1)} %broadcast_select_fusion.75) | copy-start | bytes 772
  67.2 17.2 %copy-start.124 = (bf16[2,1,1,1,64]{4,0,3,2,1:T(2,128)(2,1)}, bf16[2,1,1,1,64]{4,0,3,2,1:T(2,128)(2,1)S(1)}, u32[]{:S(2)}) copy-start(bf16[2,1,1,1,64]{4,0,3,2,1:T(2,128)(2,1)S(1)} %broadcast_select_fusion.76) | copy-start | bytes 772
  68.5 15.9 %copy-start.33 = (bf16[2,1,1,8,64]{4,0,3,2,1:T(2,128)(2,1)}, bf16[2,1,1,8,64]{4,0,3,2,1:T(2,128)(2,1)S(1)}, u32[]{:S(2)}) copy-start(bf16[2,1,1,8,64]{4,0,3,2,1:T(2,128)(2,1)S(1)} %broadcast_select_fusion.44) | copy-start | bytes 6148
  102.5 25.2 %copy-start.13 = (bf16[3,8,8,64]{3,2,1,0:T(8,128)(2,1)S(1)}, bf16[3,8,8,64]{3,2,1,0:T(8,128)(2,1)}, u32[]{:S(2)}) copy-start(bf16[3,8,8,64]{3,2,1,0:T(8,128)(2,1)} %get-tuple-element.75) | copy-start | bytes 73732
  102.5 25.9 %copy-start.12 = (bf16[3,8,8,64]{3,2,1,0:T(8,128)(2,1)S(1)}, bf16[3,8,8,64]{3,2,1,0:T(8,128)(2,1)}, u32[]{:S(2)}) copy-start(bf16[3,8,8,64]{3,2,1,0:T(8,128)(2,1)} %get-tuple-element.95) | copy-start | bytes 73732
  102.5 26.6 %copy-start.23 = (bf16[3,8,1,1,64]{4,3,2,1,0:T(2,128)(2,1)S(1)}, bf16[3,8,1,1,64]{4,3,2,1,0:T(2,128)(2,1)}, u32[]{:S(2)}) copy-start(bf16[3,8,1,1,64]{4,3,2,1,0:T(2,128)(2,1)} %get-tuple-element.71) | copy-start | bytes 9220
  102.5 27.3 %copy-start.24 = (bf16[3,8,1,1,64]{4,3,2,1,0:T(2,128)(2,1)S(1)}, bf16[3,8,1,1,64]{4,3,2,1,0:T(2,128)(2,1)}, u32[]{:S(2)}) copy-start(bf16[3,8,1,1,64]{4,3,2,1,0:T(2,128)(2,1)} %get-tuple-element.91) | copy-start | bytes 9220
  102.5 28.0 %copy-start.19 = (bf16[2,1,8,8,64]{4,3,2,1,0:T(8,128)(2,1)S(1)}, bf16[2,1,8,8,64]{4,3,2,1,0:T(8,128)(2,1)}, u32[]{:S(2)}) copy-start(bf16[2,1,8,8,64]{4,3,2,1,0:T(8,128)(2,1)} %get-tuple-element.69) | copy-start | bytes 49156
  102.5 32.3 %copy-start.20 = (bf16[2,1,8,8,64]{4,3,2,1,0:T(8,128)(2,1)S(1)}, bf16[2,1,8,8,64]{4,3,2,1,0:T(8,128)(2,1)}, u32[]{:S(2)}) copy-start(bf16[2,1,8,8,64]{4,3,2,1,0:T(8,128)(2,1)} %get-tuple-element.89) | copy-start | bytes 49156
  104.1 66.0 %collective-permute-start.7 = (bf16[1,2,8,512]{3,2,1,0:T(8,128)(2,1)}, bf16[1,2,8,512]{3,2,1,0:T(8,128)(2,1)}, u32[]{:S(2)}, u32[]{:S(2)}) collective-permute-start(bf16[1,2,8,512]{3,2,1,0:T(8,128)(2,1)} %slice.837), channel_id=1, source_target_pairs={{1,0},{2,1},{3,2},{4,3},{5,4},{6,5},{7,6},{8,7},{9,8},{10,9},{11,1... | collective-permute-start | bytes 49160 | tf_op jit(solution)/shard_map/ppermute | solution.py:20
  107.4 64.2 %collective-permute-start.3 = (bf16[1,2,8,512]{3,2,1,0:T(8,128)(2,1)}, bf16[1,2,8,512]{3,2,1,0:T(8,128)(2,1)}, u32[]{:S(2)}, u32[]{:S(2)}) collective-permute-start(bf16[1,2,8,512]{3,2,1,0:T(8,128)(2,1)} %slice.781), channel_id=1, source_target_pairs={{1,0},{2,1},{3,2},{4,3},{5,4},{6,5},{7,6},{8,7},{9,8},{10,9},{11,1... | collective-permute-start | bytes 49160 | tf_op jit(solution)/shard_map/ppermute | solution.py:20
  131.2 42.5 %collective-permute-start.6 = (bf16[1,2,8,512]{3,2,1,0:T(8,128)(2,1)}, bf16[1,2,8,512]{3,2,1,0:T(8,128)(2,1)}, u32[]{:S(2)}, u32[]{:S(2)}) collective-permute-start(bf16[1,2,8,512]{3,2,1,0:T(8,128)(2,1)} %slice.819), channel_id=1, source_target_pairs={{0,1},{1,2},{2,3},{3,4},{4,5},{5,6},{6,7},{7,8},{8,9},{9,10},{10,1... | collective-permute-start | bytes 49160 | tf_op jit(solution)/shard_map/ppermute | solution.py:17
  135.6 39.6 %collective-permute-start.2 = (bf16[1,2,8,512]{3,2,1,0:T(8,128)(2,1)}, bf16[1,2,8,512]{3,2,1,0:T(8,128)(2,1)}, u32[]{:S(2)}, u32[]{:S(2)}) collective-permute-start(bf16[1,2,8,512]{3,2,1,0:T(8,128)(2,1)} %slice.763), channel_id=1, source_target_pairs={{0,1},{1,2},{2,3},{3,4},{4,5},{5,6},{6,7},{7,8},{8,9},{9,10},{10,1... | collective-permute-start | bytes 49160 | tf_op jit(solution)/shard_map/ppermute | solution.py:17
  176.8 30.7 %copy-start.27 = (bf16[3,64]{1,0:T(4,128)(2,1)S(1)}, bf16[3,64]{1,0:T(4,128)(2,1)}, u32[]{:S(2)}) copy-start(bf16[3,64]{1,0:T(4,128)(2,1)} %get-tuple-element.110) | copy-start | bytes 1156
  176.9 31.3 %copy-start.28 = (bf16[3,64]{1,0:T(4,128)(2,1)S(1)}, bf16[3,64]{1,0:T(4,128)(2,1)}, u32[]{:S(2)}) copy-start(bf16[3,64]{1,0:T(4,128)(2,1)} %get-tuple-element.142) | copy-start | bytes 1156
  186.8 24.8 %copy-start.111 = (bf16[2,64]{1,0:T(2,128)(2,1)S(1)}, bf16[2,64]{1,0:T(2,128)(2,1)}, u32[]{:S(2)}) copy-start(bf16[2,64]{1,0:T(2,128)(2,1)} %gather_fusion.103) | copy-start | bytes 772
  186.9 24.8 %copy-start.112 = (bf16[2,64]{1,0:T(2,128)(2,1)S(1)}, bf16[2,64]{1,0:T(2,128)(2,1)}, u32[]{:S(2)}) copy-start(bf16[2,64]{1,0:T(2,128)(2,1)} %gather_fusion.51) | copy-start | bytes 772
  186.9 25.5 %copy-start.47 = (bf16[2,8,64]{2,1,0:T(8,128)(2,1)S(1)}, bf16[2,8,64]{2,1,0:T(8,128)(2,1)}, u32[]{:S(2)}) copy-start(bf16[2,8,64]{2,1,0:T(8,128)(2,1)} %gather_fusion.102) | copy-start | bytes 6148
  186.9 25.5 %copy-start.48 = (bf16[2,8,64]{2,1,0:T(8,128)(2,1)S(1)}, bf16[2,8,64]{2,1,0:T(8,128)(2,1)}, u32[]{:S(2)}) copy-start(bf16[2,8,64]{2,1,0:T(8,128)(2,1)} %gather_fusion.50) | copy-start | bytes 6148
  186.9 26.1 %copy-start.113 = (bf16[2,64]{1,0:T(2,128)(2,1)S(1)}, bf16[2,64]{1,0:T(2,128)(2,1)}, u32[]{:S(2)}) copy-start(bf16[2,64]{1,0:T(2,128)(2,1)} %gather_fusion.101) | copy-start | bytes 772
  186.9 26.1 %copy-start.114 = (bf16[2,64]{1,0:T(2,128)(2,1)S(1)}, bf16[2,64]{1,0:T(2,128)(2,1)}, u32[]{:S(2)}) copy-start(bf16[2,64]{1,0:T(2,128)(2,1)} %gather_fusion.49) | copy-start | bytes 772
  186.9 26.8 %copy-start.45 = (bf16[2,8,64]{2,1,0:T(8,128)(2,1)S(1)}, bf16[2,8,64]{2,1,0:T(8,128)(2,1)}, u32[]{:S(2)}) copy-start(bf16[2,8,64]{2,1,0:T(8,128)(2,1)} %gather_fusion.100) | copy-start | bytes 6148
  186.9 26.8 %copy-start.46 = (bf16[2,8,64]{2,1,0:T(8,128)(2,1)S(1)}, bf16[2,8,64]{2,1,0:T(8,128)(2,1)}, u32[]{:S(2)}) copy-start(bf16[2,8,64]{2,1,0:T(8,128)(2,1)} %gather_fusion.48) | copy-start | bytes 6148
  (77 other events, 419.7 us)
Sparse Core Ops, SparseCore 0:
  246.5 347.1 all-reduce.14
where the time goes:
time: 613 us; the launch traced here: 604 us
  waiting for transfers between devices  345 us (56%)
  local copies, waits for them, and re-layouts  120 us (20%)
  matrix products  48.1 us (8%)
  other arithmetic  47.4 us (8%)
  starting transfers between devices  26.3 us (4%)
  between operations  17.2 us (3%)
    psum x1, waiting for transfers between devices, on_device(): filter_first, filter_second = lax.psum((filter_first, filter_second), 'dom')  345 us
    gather x104, local copies, waits for them, and re-layouts, pad_from(): blocks[offset] = jnp.take(portion, lookup[:, number], axis=0)  78.4 us
    dot_general x54, matrix products, weight_grad(): jnp.einsum('nxyzi,nxyzo->io', window, grads, preferred_element_type=jnp.f...  30.1 us
    select_n x95, other arithmetic, pad_from(): blocks[offset] = jnp.take(portion, lookup[:, number], axis=0)  20.4 us
    conv_general_dilated x4, matrix products, convolve(): lax.conv_general_dilated(padded, kernel, (1, 1, 1), 'VALID', dimension_nu...  18.1 us
    ppermute x4, starting transfers between devices, with_halo(): lax.ppermute(lax.slice_in_dim(block, 0, width, axis=dim), axis, backward)  15.2 us
    concatenate x7, other arithmetic, join_blocks(): return jnp.concatenate(planes, axis=1)  13.3 us
  transfers between devices with their start and end apart: 9, of which 1 were waited for; matrix products, arithmetic and copies ran while one was open for 14% of the time, Pallas kernels for 0%

commit v1 on v0

v1 whole, which is shorter than its diff:
```python
import functools
import math

import jax
import jax.numpy as jnp
from jax import lax
from jax.experimental import pallas as pl
from jax.experimental.pallas import tpu as pltpu
from jax.sharding import PartitionSpec as P

C = 64
E = 8
FEAT, GOUT, MID, GHID = 0, 1, 2, 3
TN = (((0,), (0,)), ((), ()))
NT = (((1,), (1,)), ((), ()))
ROWS = 27 * C
HALF = ROWS // 2
CH = 16
NCORE = 2
NZ = 16


def entry(nb, brick, offset):
    if offset == (0, 0, 0):
        return 8 * brick
    place = (offset[0] + 1) * 9 + (offset[1] + 1) * 3 + offset[2] + 1
    ident = nb[brick, place if place < 13 else place - 1]
    return jnp.where(ident < 0, -1000, (ident & 1) * 8)


def build_selection(nb, sel):
    row = lax.broadcasted_iota(jnp.int32, (16, 160), 0)
    lane = lax.broadcasted_iota(jnp.int32, (16, 160), 1)
    y = row & 7
    second = row >= 8
    for iz in range(3):
        for c in range(3):
            yy = y + (c - 1)
            wrap = (yy < 0) | (yy > 7)
            for ix in range(3):
                codes = []
                for brick in range(2):
                    inner = entry(nb, brick, (ix - 1, 0, iz - 1))
                    if c == 1:
                        codes.append(jnp.full((16, 160), inner, jnp.int32))
                    else:
                        outer = entry(nb, brick, (ix - 1, c - 1, iz - 1))
                        codes.append(jnp.where(wrap, outer, inner))
                target = jnp.where(second, codes[1], codes[0]) + (yy & 7)
                for x in ((0,), tuple(range(1, 9)), (9,))[ix]:
                    hit = lane == target + 16 * x
                    sel[iz, 160 * c + 16 * x : 160 * c + 16 * x + 16, :] = jnp.where(
                        hit, 1.0, 0.0
                    ).astype(jnp.bfloat16)


def build_bands(weight, band, band_t):
    zero = jnp.zeros((C, C), jnp.bfloat16)
    for t in range(9):
        taps = [weight[3 * t + e] for e in range(3)]
        for zi in range(4):
            left = taps[zi] if zi < 3 else zero
            right = taps[zi - 1] if zi > 0 else zero
            band[t, C * zi : C * zi + C, :] = jnp.concatenate([left, right], axis=1)
        band_t[8 - t, :C, :] = jnp.concatenate([taps[2], taps[1], taps[0], zero], axis=1)
        band_t[8 - t, C:, :] = jnp.concatenate([zero, taps[2], taps[1], taps[0]], axis=1)


def build_padded(field, raw, sel, padded):
    source = raw[field].reshape(160, 512).astype(jnp.float32)
    source = pltpu.roll(source, C, 1).astype(jnp.bfloat16)
    edge = source[:, :128]
    low = lax.broadcasted_iota(jnp.int32, (480, 128), 1) < C
    inner = jnp.dot(sel[1], source, preferred_element_type=jnp.float32)
    before = jnp.dot(sel[0], edge, preferred_element_type=jnp.float32)
    after = jnp.dot(sel[2], edge, preferred_element_type=jnp.float32)
    padded[field, :, 128:512] = inner[:, 128:].astype(jnp.bfloat16)
    padded[field, :, :128] = jnp.where(low, before, inner[:, :128]).astype(jnp.bfloat16)
    padded[field, :, 512:] = jnp.where(low, inner[:, :128], after).astype(jnp.bfloat16)


def window(padded, field, t, pair):
    a, c = t // 3, t % 3
    start = 160 * c + 16 * a
    return padded[field, start : start + 128, 128 * pair : 128 * pair + 256]


def convolve(padded, field, band, pair, flipped):
    total = None
    for t in range(9):
        part = window(padded, field, t, pair)
        if flipped:
            term = lax.dot_general(part, band[t], NT, preferred_element_type=jnp.float32)
        else:
            term = jnp.dot(part, band[t], preferred_element_type=jnp.float32)
        total = term if total is None else total + term
    return total


def kernel(
    ny, nz, scale,
    feat, wa, wb, nb, act, cot,
    out, gfeat, fa, fb,
    raw, sel, padded, band_a, band_at, band_b, band_bt, sums, from_core, from_y, ysum, from_z, full,
    halo_send, halo_recv, core_send, core_recv, y_send, y_recv, z_send, z_recv,
    gz_send, gz_recv, gy_send, gy_recv, gc_send, gc_recv,
):
    count = ny * nz * NCORE
    me = lax.axis_index("dom")
    core = me % NCORE
    z = (me // NCORE) % nz
    y = me // (NCORE * nz)
    up = (me + 1) % count
    down = (me + count - 1) % count
    partner = me + 1 - 2 * core

    def at_y(step):
        return (((y + step) % ny) * nz + z) * NCORE + core

    def at_z(step):
        return (y * nz + (z + step) % nz) * NCORE + core

    barrier = pltpu.get_barrier_semaphore()
    pl.semaphore_signal(barrier, inc=1, device_id={"dom": up})
    pl.semaphore_signal(barrier, inc=1, device_id={"dom": down})
    for step in range(1, ny):
        pl.semaphore_signal(barrier, inc=1, device_id={"dom": at_y(step)})

    def greet(step, carry):
        pl.semaphore_signal(barrier, inc=1, device_id={"dom": at_z(step)})
        return carry

    lax.fori_loop(1, nz, greet, 0)

    keep = [jnp.where(act[b] > 0, 1.0, 0.0) for b in range(2)]
    rows = lax.broadcasted_iota(jnp.int32, (128, 128), 0)
    alive = jnp.where((rows & 8) == 0, keep[0], keep[1])
    raw[FEAT, 1:9] = jnp.concatenate(
        [feat[b].astype(jnp.float32) for b in range(2)], axis=1
    ).astype(jnp.bfloat16)
    raw[GOUT, 1:9] = jnp.concatenate(
        [cot[b].astype(jnp.float32) * keep[b] for b in range(2)], axis=1
    ).astype(jnp.bfloat16)

    def halo(number):
        copies = []
        for way, (source, target, device) in enumerate(((8, 0, up), (1, 9, down))):
            copies.append(
                pltpu.make_async_remote_copy(
                    src_ref=raw.at[2 * number : 2 * number + 2, source],
                    dst_ref=raw.at[2 * number : 2 * number + 2, target],
                    send_sem=halo_send.at[2 * number + way],
                    recv_sem=halo_recv.at[2 * number + way],
                    device_id={"dom": device},
                )
            )
        return copies

    pl.semaphore_wait(barrier, 2 + (ny - 1) + (nz - 1))
    first = halo(0)
    for copy in first:
        copy.start()
    build_selection(nb, sel)
    build_bands(wa, band_a, band_at)
    build_bands(wb, band_b, band_bt)
    for copy in first:
        copy.wait()

    build_padded(FEAT, raw, sel, padded)
    build_padded(GOUT, raw, sel, padded)
    for pair in range(4):
        lanes = slice(128 * pair, 128 * pair + 128)
        hidden = convolve(padded, FEAT, band_a, pair, False)
        grad = convolve(padded, GOUT, band_bt, pair, True)
        s = jax.nn.sigmoid(hidden)
        middle = alive * (hidden * s)
        ghid = grad * (s * (1.0 + hidden * (1.0 - s)))
        raw[MID, 1:9, :, lanes] = middle.astype(jnp.bfloat16).reshape(8, 16, 128)
        raw[GHID, 1:9, :, lanes] = ghid.astype(jnp.bfloat16).reshape(8, 16, 128)
    second = halo(1)
    for copy in second:
        copy.start()

    low = lax.broadcasted_iota(jnp.int32, (C, 128), 1) < C
    for t in range(9):
        one = None
        two = None
        for pair in range(4):
            lanes = slice(128 * pair, 128 * pair + 128)
            ghid = raw[GHID, 1:9, :, lanes].reshape(128, 128)
            middle = raw[MID, 1:9, :, lanes].reshape(128, 128)
            term = lax.dot_general(
                window(padded, FEAT, t, pair), ghid, TN, preferred_element_type=jnp.float32
            )
            one = term if one is None else one + term
            term = lax.dot_general(
                middle, window(padded, GOUT, 8 - t, pair), TN, preferred_element_type=jnp.float32
            )
            two = term if two is None else two + term
        straight = two[:C]
        moved = two[C:]
        for e in range(3):
            near = one[C * e : C * e + C]
            far = one[C * e + C : C * e + 2 * C]
            flip = 2 - e
            pieces = []
            for value, block in ((straight, flip), (moved, flip + 1)):
                tile = value[:, 128 * (block // 2) : 128 * (block // 2) + 128]
                pieces.append(tile if block % 2 else pltpu.roll(tile, C, 1))
            first_part = near + pltpu.roll(far, C, 1)
            second_part = pieces[0] + pieces[1]
            start = 192 * t + C * e
            sums[start : start + C, :] = jnp.where(low, first_part, second_part)

    own = pl.multiple_of(core * HALF, 8)
    other = pl.multiple_of((1 - core) * HALF, 8)
    to_core = pltpu.make_async_remote_copy(
        src_ref=sums.at[pl.ds(other, HALF)],
        dst_ref=from_core,
        send_sem=core_send,
        recv_sem=core_recv,
        device_id={"dom": partner},
    )
    to_core.start()
    for copy in second:
        copy.wait()
    build_padded(MID, raw, sel, padded)
    build_padded(GHID, raw, sel, padded)
    to_core.wait()
    ylen = HALF // ny
    from_core[...] = from_core[...] + sums[pl.ds(own, HALF), :]

    y_copies = []
    for step in range(1, ny):
        begin = pl.multiple_of(((y + step) % ny) * ylen, 8)
        y_copies.append(
            pltpu.make_async_remote_copy(
                src_ref=from_core.at[pl.ds(begin, ylen)],
                dst_ref=from_y.at[step - 1],
                send_sem=y_send.at[step - 1],
                recv_sem=y_recv.at[step - 1],
                device_id={"dom": at_y(step)},
            )
        )
    for copy in y_copies:
        copy.start()

    def last(field, band, flipped, target, base, masked):
        for pair in range(4):
            lanes = slice(128 * pair, 128 * pair + 128)
            value = convolve(padded, field, band, pair, flipped)
            if masked:
                value = value * alive
            value = value.reshape(8, 16, 128)
            for b in range(2):
                given = base[b, :, :, lanes].astype(jnp.float32)
                if masked:
                    given = given * keep[b]
                target[b, :, :, lanes] = (given + value[:, 8 * b : 8 * b + 8]).astype(jnp.bfloat16)

    last(MID, band_b, False, out, feat, False)
    for copy in y_copies:
        copy.wait()
    mine = pl.multiple_of(y * ylen, 8)
    total = from_core[pl.ds(mine, ylen), :]
    for step in range(1, ny):
        total = total + from_y[step - 1]
    ysum[:ylen, :] = total
    if ylen < CH * nz:
        ysum[ylen:, :] = jnp.zeros((CH * nz - ylen, 128), jnp.float32)

    def z_copy(step):
        begin = pl.multiple_of(((z + step) % nz) * CH, CH)
        return pltpu.make_async_remote_copy(
            src_ref=ysum.at[pl.ds(begin, CH)],
            dst_ref=from_z.at[step - 1],
            send_sem=z_send.at[step - 1],
            recv_sem=z_recv.at[step - 1],
            device_id={"dom": at_z(step)},
        )

    def g_copy(step):
        return pltpu.make_async_remote_copy(
            src_ref=full.at[core, y, z],
            dst_ref=full.at[core, y, z],
            send_sem=gz_send.at[step - 1],
            recv_sem=gz_recv.at[step - 1],
            device_id={"dom": at_z(step)},
        )

    def start_all(make):
        def body(step, carry):
            make(step).start()
            return carry

        lax.fori_loop(1, nz, body, 0)

    def wait_all(make):
        def body(step, carry):
            make(step).wait()
            return carry

        lax.fori_loop(1, nz, body, 0)

    start_all(z_copy)
    last(GHID, band_at, True, gfeat, cot, True)
    wait_all(z_copy)
    total = ysum[pl.ds(pl.multiple_of(z * CH, CH), CH), :]
    for step in range(1, nz):
        total = total + from_z[step - 1]
    full[core, y, z] = (total * scale).astype(jnp.bfloat16)
    start_all(g_copy)
    wait_all(g_copy)

    gy_copies = []
    for step in range(1, ny):
        gy_copies.append(
            pltpu.make_async_remote_copy(
                src_ref=full.at[core, y],
                dst_ref=full.at[core, y],
                send_sem=gy_send.at[step - 1],
                recv_sem=gy_recv.at[step - 1],
                device_id={"dom": at_y(step)},
            )
        )
    for copy in gy_copies:
        copy.start()
    for copy in gy_copies:
        copy.wait()
    gc_copy = pltpu.make_async_remote_copy(
        src_ref=full.at[core],
        dst_ref=full.at[core],
        send_sem=gc_send,
        recv_sem=gc_recv,
        device_id={"dom": partner},
    )
    gc_copy.start()
    gc_copy.wait()
    for h in range(NCORE):
        for j in range(ny):
            value = full[h, j].reshape(CH * nz, 128)[:ylen, :].astype(jnp.float32)
            begin = h * HALF + j * ylen
            fa[begin : begin + ylen, :] = value[:, :C]
            fb[begin : begin + ylen, :] = pltpu.roll(value, C, 1)[:, :C]


def on_device(ny, nz, features, weight_first, weight_second, neighbours, active, cotangent):
    count = ny * nz * NCORE
    scale = 1.0 / math.sqrt(2 * count * E**3)
    vmem = pl.BlockSpec(memory_space=pltpu.VMEM)
    smem = pl.BlockSpec(memory_space=pltpu.SMEM)
    bf16, f32 = jnp.bfloat16, jnp.float32
    dma = pltpu.SemaphoreType.DMA
    out, gfeat, fa, fb = pl.pallas_call(
        functools.partial(kernel, ny, nz, scale),
        out_shape=(
            jax.ShapeDtypeStruct(features.shape, bf16),
            jax.ShapeDtypeStruct(features.shape, bf16),
            jax.ShapeDtypeStruct((ROWS, C), f32),
            jax.ShapeDtypeStruct((ROWS, C), f32),
        ),
        in_specs=[vmem, vmem, vmem, smem, smem, vmem],
        out_specs=(vmem, vmem, vmem, vmem),
        scratch_shapes=[
            pltpu.VMEM((4, 10, 16, 512), bf16),
            pltpu.VMEM((3, 480, 160), bf16),
            pltpu.VMEM((4, 480, 640), bf16),
            pltpu.VMEM((9, 256, 128), bf16),
            pltpu.VMEM((9, 128, 256), bf16),
            pltpu.VMEM((9, 256, 128), bf16),
            pltpu.VMEM((9, 128, 256), bf16),
            pltpu.VMEM((ROWS, 128), f32),
            pltpu.VMEM((HALF, 128), f32),
            pltpu.VMEM((ny - 1, HALF // ny, 128), f32),
            pltpu.VMEM((CH * nz, 128), f32),
            pltpu.VMEM((nz - 1, CH, 128), f32),
            pltpu.VMEM((NCORE, ny, nz, CH, 128), bf16),
            dma((4,)), dma((4,)),
            dma, dma,
            dma((ny - 1,)), dma((ny - 1,)),
            dma((nz - 1,)), dma((nz - 1,)),
            dma((nz - 1,)), dma((nz - 1,)),
            dma((ny - 1,)), dma((ny - 1,)),
            dma, dma,
        ],
        compiler_params=pltpu.CompilerParams(
            collective_id=0, has_side_effects=True, vmem_limit_bytes=40 * 2**20
        ),
    )(
        features,
        weight_first.reshape(27, C, C),
        weight_second.reshape(27, C, C),
        neighbours,
        active,
        cotangent,
    )
    return out, gfeat, fa.reshape(3, 3, 3, C, C), fb.reshape(3, 3, 3, C, C)


def solution(mesh):
    count = mesh.shape["dom"]
    return jax.shard_map(
        functools.partial(on_device, count // (NZ * NCORE), NZ),
        mesh=mesh,
        in_specs=(
            P(("scene", "dom"), None, None, None),
            P(),
            P(),
            P(("scene", "dom"), None),
            P(("scene", "dom")),
            P(("scene", "dom"), None, None, None),
        ),
        out_specs=(
            P(("scene", "dom"), None, None, None),
            P(("scene", "dom"), None, None, None),
            P("scene", None, None, None, None),
            P("scene", None, None, None, None),
        ),
        check_vma=False,
    )
```

time: 613 us -> 66 us (0.11); the launches traced: 604 us -> 65.7 us
  waiting for transfers between devices: 345 us -> 0 us
  local copies, waits for them, and re-layouts: 120 us -> 7.63 us
  Pallas kernels: 0 us -> 57.4 us
  matrix products: 48.1 us -> 0 us
  other arithmetic: 47.4 us -> 0 us
  starting transfers between devices: 26.3 us -> 0 us
  between operations: 17.2 us -> 0.66 us
    psum x1 -> x0, waiting for transfers between devices: 345 us -> none  [on_device(): filter_first, filter_second = lax.psum((filter_first, filter_second), 'dom')]
    gather x104 -> x0, local copies, waits for them, and re-layouts: 78.4 us -> none  [pad_from(): blocks[offset] = jnp.take(portion, lookup[:, number], axis=0)]
    pallas_call x0 -> x1, Pallas kernels: none -> 57.4 us  [on_device(): pl.pallas_call(functools.partial(kernel, ny, nz, scale), out_shape=(jax.S...]
    dot_general x54 -> x0, matrix products: 30.1 us -> none  [weight_grad(): jnp.einsum('nxyzi,nxyzo->io', window, grads, preferred_element_type=jnp.f...]
    ppermute x8 -> x0, starting transfers between devices: 26.3 us -> none  [the longest x4 15.2 us: with_halo(): lax.ppermute(lax.slice_in_dim(block, 0, width, axis=dim), axis, backward)]
    select_n x96 -> x0, other arithmetic: 20.4 us -> none  [the longest x95 20.4 us: pad_from(): blocks[offset] = jnp.take(portion, lookup[:, number], axis=0)]
    conv_general_dilated x4 -> x0, matrix products: 18.1 us -> none  [convolve(): lax.conv_general_dilated(padded, kernel, (1, 1, 1), 'VALID', dimension_nu...]
    slice x24 -> x0, local copies, waits for them, and re-layouts: 17.7 us -> none  [the longest x4 7.88 us: weight_grad(): padded[:, shift_x:shift_x + E, shift_y:shift_y + E, shift_z:shift_z + E]]
  transfers between devices with their start and end apart: 9 -> 0, of which waited for: 1 -> 0; matrix products, arithmetic and copies ran while one was open for 14% -> 0% of each run, Pallas kernels for 0% -> 0%
where the time goes in v1:
time: 66 us; the launch traced here: 65.7 us
  Pallas kernels  57.4 us (87%)
  local copies, waits for them, and re-layouts  7.63 us (12%)
  between operations  0.66 us (1%)
    pallas_call x1, Pallas kernels, on_device(): pl.pallas_call(functools.partial(kernel, ny, nz, scale), out_shape=(jax.S...  57.4 us
    unnamed x16, local copies, waits for them, and re-layouts  7.63 us

profile of v1, /device:TPU:1, one launch (start us, length us, event | category | flops | bytes accessed | tf_op | source)
XLA Modules:
  0.0 65.7 jit_solution(13472612648636269824)
XLA Ops:
  0.6 0.0 copy-start.4
  0.6 0.0 copy-start.5
  0.7 0.7 %copy-done.4 = s32[2,26]{1,0:T(2,128)S(1)} copy-done((s32[2,26]{1,0:T(2,128)S(1)}, s32[2,26]{1,0:T(2,128)}, u32[]{:S(2)}) %copy-start.4) | copy-done | bytes 232
  1.3 0.0 copy-done.5
  1.3 0.0 copy-start
  1.3 1.0 %copy-done = bf16[3,3,3,64,64]{4,3,2,1,0:T(8,128)(2,1)S(1)} copy-done((bf16[3,3,3,64,64]{4,3,2,1,0:T(8,128)(2,1)S(1)}, bf16[3,3,3,64,64]{4,3,2,1,0:T(8,128)(2,1)}, u32[]{:S(2)}) %copy-start) | copy-done | bytes 221208
  2.3 0.0 copy-start.1
  2.3 1.0 %copy-done.1 = bf16[3,3,3,64,64]{4,3,2,1,0:T(8,128)(2,1)S(1)} copy-done((bf16[3,3,3,64,64]{4,3,2,1,0:T(8,128)(2,1)S(1)}, bf16[3,3,3,64,64]{4,3,2,1,0:T(8,128)(2,1)}, u32[]{:S(2)}) %copy-start.1) | copy-done | bytes 221208
  3.3 0.0 copy-start.2
  3.3 0.9 %copy-done.2 = bf16[2,8,8,512]{3,2,1,0:T(8,128)(2,1)S(1)} copy-done((bf16[2,8,8,512]{3,2,1,0:T(8,128)(2,1)S(1)}, bf16[2,8,8,512]{3,2,1,0:T(8,128)(2,1)}, u32[]{:S(2)}) %copy-start.2) | copy-done | bytes 131096
  4.2 0.0 copy-start.3
  4.2 0.9 %copy-done.3 = bf16[2,8,8,512]{3,2,1,0:T(8,128)(2,1)S(1)} copy-done((bf16[2,8,8,512]{3,2,1,0:T(8,128)(2,1)S(1)}, bf16[2,8,8,512]{3,2,1,0:T(8,128)(2,1)}, u32[]{:S(2)}) %copy-start.3) | copy-done | bytes 131096
  5.2 57.4 %shard_map.93 = (bf16[2,8,8,512]{3,2,1,0:T(8,128)(2,1)S(1)}, bf16[2,8,8,512]{3,2,1,0:T(8,128)(2,1)S(1)}, f32[1728,64]{1,0:T(8,128)S(1)}, f32[1728,64]{1,0:T(8,128)S(1)}) custom-call(bf16[2,8,8,512]{3,2,1,0:T(8,128)(2,1)S(1)} %copy-done.2, bf16[27,64,64]{2,1,0:T(8,128)(2,1)S(1)} %bitcast.6, bf16[27,64,64]{2,1,0:T(8,128)(2,1)S(1)} %bitcast.7, ...), custom_call_target="tpu_custom_call" | custom-call | tf_op jit(solution)/shard_map/pallas_call | solution.py:354
  62.6 0.7 %copy.14 = bf16[2,8,8,512]{3,2,1,0:T(8,128)(2,1)} copy(bf16[2,8,8,512]{3,2,1,0:T(8,128)(2,1)S(1)} %get-tuple-element.16) | data formatting | bytes 262144
  63.3 0.7 copy.15
  63.9 0.9 %copy.16 = f32[3,3,3,64,64]{4,3,2,1,0:T(8,128)} copy(f32[3,3,3,64,64]{4,3,2,1,0:T(8,128)S(1)} %bitcast.5) | data formatting | bytes 884736
  64.8 0.9 %copy.17 = f32[3,3,3,64,64]{4,3,2,1,0:T(8,128)} copy(f32[3,3,3,64,64]{4,3,2,1,0:T(8,128)S(1)} %bitcast.4) | data formatting | bytes 884736
Async XLA Ops:
  0.6 0.7 %copy-start.4 = (s32[2,26]{1,0:T(2,128)S(1)}, s32[2,26]{1,0:T(2,128)}, u32[]{:S(2)}) copy-start(s32[2,26]{1,0:T(2,128)} %nb.1) | copy-start | bytes 628
  0.6 0.7 %copy-start.5 = (s32[2]{0:T(128)S(1)}, s32[2]{0:T(128)}, u32[]{:S(2)}) copy-start(s32[2]{0:T(128)} %act.1) | copy-start | bytes 28
  1.3 1.0 %copy-start = (bf16[3,3,3,64,64]{4,3,2,1,0:T(8,128)(2,1)S(1)}, bf16[3,3,3,64,64]{4,3,2,1,0:T(8,128)(2,1)}, u32[]{:S(2)}) copy-start(bf16[3,3,3,64,64]{4,3,2,1,0:T(8,128)(2,1)} %param.7) | copy-start | bytes 663556
  2.3 1.0 %copy-start.1 = (bf16[3,3,3,64,64]{4,3,2,1,0:T(8,128)(2,1)S(1)}, bf16[3,3,3,64,64]{4,3,2,1,0:T(8,128)(2,1)}, u32[]{:S(2)}) copy-start(bf16[3,3,3,64,64]{4,3,2,1,0:T(8,128)(2,1)} %param.8) | copy-start | bytes 663556
  3.3 0.9 %copy-start.2 = (bf16[2,8,8,512]{3,2,1,0:T(8,128)(2,1)S(1)}, bf16[2,8,8,512]{3,2,1,0:T(8,128)(2,1)}, u32[]{:S(2)}) copy-start(bf16[2,8,8,512]{3,2,1,0:T(8,128)(2,1)} %feat.1) | copy-start | bytes 393220
  4.2 0.9 %copy-start.3 = (bf16[2,8,8,512]{3,2,1,0:T(8,128)(2,1)S(1)}, bf16[2,8,8,512]{3,2,1,0:T(8,128)(2,1)}, u32[]{:S(2)}) copy-start(bf16[2,8,8,512]{3,2,1,0:T(8,128)(2,1)} %cot.1) | copy-start | bytes 393220

commit v2 on v1

v2 whole, which is shorter than its diff:
```python
import functools
import math

import jax
import jax.numpy as jnp
from jax import lax
from jax.experimental import pallas as pl
from jax.experimental.pallas import tpu as pltpu
from jax.sharding import PartitionSpec as P

C = 64
E = 8
FEAT, GOUT, MID, GHID = 0, 1, 2, 3
TN = (((0,), (0,)), ((), ()))
NT = (((1,), (1,)), ((), ()))
ROWS = 27 * C
HALF = ROWS // 2
NCORE = 2
NZ = 16
ZLOW = 4
CH = 64
F32 = jnp.float32
BF16 = jnp.bfloat16


def entry(nb, brick, offset):
    if offset == (0, 0, 0):
        return 8 * brick
    place = (offset[0] + 1) * 9 + (offset[1] + 1) * 3 + offset[2] + 1
    ident = nb[brick, place if place < 13 else place - 1]
    return jnp.where(ident < 0, -1000, (ident & 1) * 8)


def build_selection(nb, sel, sel_edge):
    row = lax.broadcasted_iota(jnp.int32, (16, 128), 0)
    lane = lax.broadcasted_iota(jnp.int32, (16, 128), 1)
    y = row & 7
    second = row >= 8
    for iz in range(3):
        for c in range(3):
            yy = y + (c - 1)
            wrap = (yy < 0) | (yy > 7)
            for ix in range(3):
                codes = []
                for brick in range(2):
                    inner = entry(nb, brick, (ix - 1, 0, iz - 1))
                    if c == 1:
                        codes.append(jnp.full((16, 128), inner, jnp.int32))
                    else:
                        outer = entry(nb, brick, (ix - 1, c - 1, iz - 1))
                        codes.append(jnp.where(wrap, outer, inner))
                target = jnp.where(second, codes[1], codes[0]) + (yy & 7)
                if ix == 1:
                    for x in range(8):
                        hit = jnp.where(lane == target + 16 * x, 1.0, 0.0).astype(BF16)
                        sel[iz, 128 * c + 16 * x : 128 * c + 16 * x + 16, :] = hit
                else:
                    side = ix // 2
                    hit = jnp.where(lane == target + 16 * side, 1.0, 0.0).astype(BF16)
                    sel_edge[iz, 32 * c + 16 * side : 32 * c + 16 * side + 16, :] = hit[:, :32]


def build_bands(weight, band, band_t):
    zero = jnp.zeros((C, C), BF16)
    for t in range(9):
        taps = [weight[t // 3, t % 3, e] for e in range(3)]
        for zi in range(4):
            left = taps[zi] if zi < 3 else zero
            right = taps[zi - 1] if zi > 0 else zero
            band[t, C * zi : C * zi + C, :] = jnp.concatenate([left, right], axis=1)
        band_t[8 - t, :C, :] = jnp.concatenate([taps[2], taps[1], taps[0], zero], axis=1)
        band_t[8 - t, C:, :] = jnp.concatenate([zero, taps[2], taps[1], taps[0]], axis=1)


def select(source, choose):
    rows = choose.shape[1]
    low = lax.broadcasted_iota(jnp.int32, (rows, 128), 1) < C
    source = pltpu.roll(source.astype(F32), C, 1).astype(BF16)
    edge = source[:, :128]
    inner = jnp.dot(choose[1], source, preferred_element_type=F32)
    before = jnp.dot(choose[0], edge, preferred_element_type=F32)
    after = jnp.dot(choose[2], edge, preferred_element_type=F32)
    first = jnp.where(low, before, inner[:, :128])
    last = jnp.where(low, inner[:, :128], after)
    return jnp.concatenate([first, inner[:, 128:], last], axis=1).astype(BF16)


def pad_inner(field, raw, sel, padded):
    value = select(raw[field, 1:9].reshape(128, 512), sel)
    for c in range(3):
        start = 160 * c + 16
        padded[field, start : start + 128, :] = value[128 * c : 128 * c + 128]


def pad_edge(field, raw, sel_edge, padded):
    source = jnp.concatenate([raw[field, 0], raw[field, 9]], axis=0)
    value = select(source, sel_edge)
    for c in range(3):
        padded[field, 160 * c : 160 * c + 16, :] = value[32 * c : 32 * c + 16]
        padded[field, 160 * c + 144 : 160 * c + 160, :] = value[32 * c + 16 : 32 * c + 32]


def multiply(part, tap, flipped):
    if flipped:
        return lax.dot_general(part, tap, NT, preferred_element_type=F32)
    return jnp.dot(part, tap, preferred_element_type=F32)


def convolve(padded, field, band, pair, flipped):
    total = None
    for t in range(9):
        start = 160 * (t % 3) + 16 * (t // 3)
        part = padded[field, start : start + 128, 128 * pair : 128 * pair + 256]
        term = multiply(part, band[t], flipped)
        total = term if total is None else total + term
    return total


def convolve_edge(padded, field, band, flipped):
    sides = []
    for layer, a in ((0, 0), (9, 2)):
        total = None
        for c in range(3):
            start = 160 * c + 16 * layer
            part = jnp.concatenate(
                [
                    padded[field, start : start + 16, 128 * pair : 128 * pair + 256]
                    for pair in range(4)
                ],
                axis=0,
            )
            term = multiply(part, band[3 * a + c], flipped)
            total = term if total is None else total + term
        sides.append(total)
    return sides


def filter_taps(t, raw, padded, sums):
    low = lax.broadcasted_iota(jnp.int32, (C, 128), 1) < C
    one = None
    two = None
    at_one = pl.multiple_of(160 * (t % 3) + 16 * (t // 3), 16)
    back = 8 - t
    at_two = pl.multiple_of(160 * (back % 3) + 16 * (back // 3), 16)
    for pair in range(4):
        lanes = slice(128 * pair, 128 * pair + 128)
        wide = slice(128 * pair, 128 * pair + 256)
        ghid = raw[GHID, 1:9, :, lanes].reshape(128, 128)
        middle = raw[MID, 1:9, :, lanes].reshape(128, 128)
        term = lax.dot_general(
            padded[FEAT, pl.ds(at_one, 128), wide], ghid, TN, preferred_element_type=F32
        )
        one = term if one is None else one + term
        term = lax.dot_general(
            middle, padded[GOUT, pl.ds(at_two, 128), wide], TN, preferred_element_type=F32
        )
        two = term if two is None else two + term
    for e in range(3):
        near = one[C * e : C * e + C]
        far = one[C * e + C : C * e + 2 * C]
        pieces = []
        for value, block in ((two[:C], 2 - e), (two[C:], 3 - e)):
            tile = value[:, 128 * (block // 2) : 128 * (block // 2) + 128]
            pieces.append(tile if block % 2 else pltpu.roll(tile, C, 1))
        first_part = near + pltpu.roll(far, C, 1)
        second_part = pieces[0] + pieces[1]
        start = pl.multiple_of(192 * t + C * e, C)
        sums[pl.ds(start, C), :] = jnp.where(low, first_part, second_part)


def kernel(
    ny, nz, scale,
    feat_in, wa_in, wb_in, nb_in, act_in, cot_in,
    out, gfeat, full,
    feat, cot, wa, wb, nb, act,
    raw, sel, sel_edge, padded, band_a, band_at, band_b, band_bt,
    sums, from_core, chip, from_plane, groups,
    in_sem, halo_send, halo_recv, core_send, core_recv, plane_send, plane_recv,
    group_send, group_recv, back_send, back_recv, last_send, last_recv,
):
    count = ny * nz * NCORE
    nhigh = nz // ZLOW
    me = lax.axis_index("dom")
    core = me % NCORE
    z = (me // NCORE) % nz
    y = me // (NCORE * nz)
    zlow = z % ZLOW
    zhigh = z // ZLOW
    spot = y * ZLOW + zlow
    up = (me + 1) % count
    down = (me + count - 1) % count
    partner = me + 1 - 2 * core
    plan = []
    for dy in range(ny - 1, -1, -1):
        for dz in range(ZLOW - 1, -1, -1):
            if dy or dz:
                plan.append((dy, dz))

    def at_plane(step):
        ty = (y + step[0]) % ny
        tz = (zlow + step[1]) % ZLOW
        return ty * ZLOW + tz, (ty * nz + zhigh * ZLOW + tz) * NCORE + core

    def at_group(step):
        return (y * nz + ((zhigh + step) % nhigh) * ZLOW + zlow) * NCORE + core

    raw[:, 0] = jnp.zeros((4, 16, 512), BF16)
    raw[:, 9] = jnp.zeros((4, 16, 512), BF16)
    barrier = pltpu.get_barrier_semaphore()
    pl.semaphore_signal(barrier, inc=1, device_id={"dom": up})
    pl.semaphore_signal(barrier, inc=1, device_id={"dom": down})
    for step in plan:
        pl.semaphore_signal(barrier, inc=1, device_id={"dom": at_plane(step)[1]})
    for step in range(1, nhigh):
        pl.semaphore_signal(barrier, inc=1, device_id={"dom": at_group(step)})

    loads = [
        pltpu.make_async_copy(source, target, in_sem.at[i])
        for i, (source, target) in enumerate(
            ((nb_in, nb), (act_in, act), (feat_in, feat), (cot_in, cot), (wa_in, wa), (wb_in, wb))
        )
    ]
    for load in loads:
        load.start()
    for field in (FEAT, GOUT):
        for c in range(3):
            padded[field, 160 * c : 160 * c + 16, :] = jnp.zeros((16, 640), BF16)
            padded[field, 160 * c + 144 : 160 * c + 160, :] = jnp.zeros((16, 640), BF16)
    chip[HALF:, :] = jnp.zeros((CH * ny * ZLOW - HALF, 128), BF16)
    for load in loads[:4]:
        load.wait()
    keep = [jnp.where(act[b] > 0, 1.0, 0.0) for b in range(2)]
    rows = lax.broadcasted_iota(jnp.int32, (128, 128), 0)
    alive = jnp.where((rows & 8) == 0, keep[0], keep[1])
    raw[FEAT, 1:9] = jnp.concatenate(
        [feat[b].astype(F32) for b in range(2)], axis=1
    ).astype(BF16)
    raw[GOUT, 1:9] = jnp.concatenate(
        [cot[b].astype(F32) * keep[b] for b in range(2)], axis=1
    ).astype(BF16)

    def halo(number):
        fields = slice(2 * number, 2 * number + 2)
        return [
            pltpu.make_async_remote_copy(
                src_ref=raw.at[fields, source],
                dst_ref=raw.at[fields, target],
                send_sem=halo_send.at[2 * number + way],
                recv_sem=halo_recv.at[2 * number + way],
                device_id={"dom": device},
            )
            for way, (source, target, device) in enumerate(((8, 0, up), (1, 9, down)))
        ]

    def halo_start(copies):
        @pl.when(me < count - 1)
        def _():
            copies[0].start()

        @pl.when(me > 0)
        def _():
            copies[1].start()

    def halo_wait(copies):
        @pl.when(me < count - 1)
        def _():
            copies[0].wait_send()
            copies[1].wait_recv()

        @pl.when(me > 0)
        def _():
            copies[1].wait_send()
            copies[0].wait_recv()

    pl.semaphore_wait(barrier, 2 + len(plan) + nhigh - 1)
    first = halo(0)
    halo_start(first)
    build_selection(nb, sel, sel_edge)
    pad_inner(FEAT, raw, sel, padded)
    pad_inner(GOUT, raw, sel, padded)
    for load in loads[4:]:
        load.wait()
    build_bands(wa, band_a, band_at)
    build_bands(wb, band_b, band_bt)
    hidden = [convolve(padded, FEAT, band_a, pair, False) for pair in range(4)]
    grad = [convolve(padded, GOUT, band_bt, pair, True) for pair in range(4)]
    halo_wait(first)
    pad_edge(FEAT, raw, sel_edge, padded)
    pad_edge(GOUT, raw, sel_edge, padded)
    hidden_edge = convolve_edge(padded, FEAT, band_a, False)
    grad_edge = convolve_edge(padded, GOUT, band_bt, True)
    for pair in range(4):
        lanes = slice(128 * pair, 128 * pair + 128)
        some = slice(16 * pair, 16 * pair + 16)

        def joined(value, sides):
            return jnp.concatenate(
                [value[:16] + sides[0][some], value[16:112], value[112:] + sides[1][some]], axis=0
            )

        h = joined(hidden[pair], hidden_edge)
        g = joined(grad[pair], grad_edge)
        s = jax.nn.sigmoid(h)
        middle = alive * (h * s)
        ghid = g * (s * (1.0 + h * (1.0 - s)))
        raw[MID, 1:9, :, lanes] = middle.astype(BF16).reshape(8, 16, 128)
        raw[GHID, 1:9, :, lanes] = ghid.astype(BF16).reshape(8, 16, 128)
    second = halo(1)
    halo_start(second)

    for i in range(5):
        filter_taps(4 * (1 - core) + i, raw, padded, sums)
    own = pl.multiple_of(core * HALF, 8)
    other = pl.multiple_of((1 - core) * HALF, 8)
    to_core = pltpu.make_async_remote_copy(
        src_ref=sums.at[pl.ds(other, HALF)],
        dst_ref=from_core,
        send_sem=core_send,
        recv_sem=core_recv,
        device_id={"dom": partner},
    )
    to_core.start()
    for i in range(4):
        filter_taps(5 * core + i, raw, padded, sums)
    to_core.wait_recv()
    from_core[...] = from_core[...] + sums[pl.ds(own, HALF), :]
    chip[:HALF, :] = from_core[...].astype(BF16)

    to_plane = []
    for i, step in enumerate(plan):
        spot_to, device = at_plane(step)
        begin = pl.multiple_of(spot_to * CH, CH)
        to_plane.append(
            pltpu.make_async_remote_copy(
                src_ref=chip.at[pl.ds(begin, CH)],
                dst_ref=from_plane.at[i],
                send_sem=plane_send.at[i],
                recv_sem=plane_recv.at[i],
                device_id={"dom": device},
            )
        )
    for copy in to_plane:
        copy.start()

    def last(field, band, flipped, target, base, masked):
        for pair in range(4):
            lanes = slice(128 * pair, 128 * pair + 128)
            value = convolve(padded, field, band, pair, flipped)
            if masked:
                value = value * alive
            value = value.reshape(8, 16, 128)
            for b in range(2):
                given = base[b, :, :, lanes].astype(F32)
                if masked:
                    given = given * keep[b]
                target[b, :, :, lanes] = (given + value[:, 8 * b : 8 * b + 8]).astype(BF16)

    halo_wait(second)
    for field in (MID, GHID):
        pad_inner(field, raw, sel, padded)
        pad_edge(field, raw, sel_edge, padded)
    last(MID, band_b, False, out, feat, False)

    total = chip[pl.ds(pl.multiple_of(spot * CH, CH), CH), :].astype(F32)
    for copy in to_plane:
        copy.wait_recv()
    for i in range(len(plan)):
        total = total + from_plane[i].astype(F32)
    groups[zhigh] = total
    to_group = [
        pltpu.make_async_remote_copy(
            src_ref=groups.at[zhigh],
            dst_ref=groups.at[zhigh],
            send_sem=group_send.at[step - 1],
            recv_sem=group_recv.at[step - 1],
            device_id={"dom": at_group(step)},
        )
        for step in range(1, nhigh)
    ]
    for copy in to_group:
        copy.start()
    last(GHID, band_at, True, gfeat, cot, True)
    for copy in to_group:
        copy.wait_recv()
    total = groups[0]
    for i in range(1, nhigh):
        total = total + groups[i]
    full[core, spot] = (total * scale).astype(BF16)
    back = [
        pltpu.make_async_remote_copy(
            src_ref=full.at[core, spot],
            dst_ref=full.at[core, spot],
            send_sem=back_send.at[i],
            recv_sem=back_recv.at[i],
            device_id={"dom": at_plane(step)[1]},
        )
        for i, step in enumerate(plan)
    ]
    for copy in back:
        copy.start()
    to_core.wait_send()
    for copy in to_plane + to_group:
        copy.wait_send()
    for copy in back:
        copy.wait_recv()
    to_last = pltpu.make_async_remote_copy(
        src_ref=full.at[core],
        dst_ref=full.at[core],
        send_sem=last_send,
        recv_sem=last_recv,
        device_id={"dom": partner},
    )
    to_last.start()
    for copy in back:
        copy.wait_send()
    to_last.wait()


def finish(out_in, gfeat_in, full, out, gfeat, fa, fb, fa_here, fb_here, sems):
    copies = [
        pltpu.make_async_copy(source, target, sems.at[i])
        for i, (source, target) in enumerate(
            ((out_in, out), (gfeat_in, gfeat), (fa_here, fa), (fb_here, fb))
        )
    ]
    copies[0].start()
    copies[1].start()
    for h in range(NCORE):
        value = full[h].reshape(full.shape[1] * CH, 128)[:HALF].astype(F32)
        fa_here[h * HALF : h * HALF + HALF, :] = value[:, :C]
        fb_here[h * HALF : h * HALF + HALF, :] = pltpu.roll(value, C, 1)[:, :C]
    copies[2].start()
    copies[3].start()
    for copy in copies:
        copy.wait()


def on_device(ny, nz, features, weight_first, weight_second, neighbours, active, cotangent):
    count = ny * nz * NCORE
    scale = 1.0 / math.sqrt(2 * count * E**3)
    plane = ny * ZLOW
    nhigh = nz // ZLOW
    vmem = pl.BlockSpec(memory_space=pltpu.VMEM)
    hbm = pl.BlockSpec(memory_space=pltpu.HBM)
    dma = pltpu.SemaphoreType.DMA
    brick = jax.ShapeDtypeStruct(features.shape, BF16)
    out, gfeat, full = pl.pallas_call(
        functools.partial(kernel, ny, nz, scale),
        out_shape=(brick, brick, jax.ShapeDtypeStruct((NCORE, plane, CH, 128), BF16)),
        in_specs=[hbm] * 6,
        out_specs=(vmem, vmem, vmem),
        scratch_shapes=[
            pltpu.VMEM(features.shape, BF16),
            pltpu.VMEM(features.shape, BF16),
            pltpu.VMEM(weight_first.shape, BF16),
            pltpu.VMEM(weight_first.shape, BF16),
            pltpu.SMEM(neighbours.shape, jnp.int32),
            pltpu.SMEM(active.shape, jnp.int32),
            pltpu.VMEM((4, 10, 16, 512), BF16),
            pltpu.VMEM((3, 384, 128), BF16),
            pltpu.VMEM((3, 96, 32), BF16),
            pltpu.VMEM((4, 480, 640), BF16),
            pltpu.VMEM((9, 256, 128), BF16),
            pltpu.VMEM((9, 128, 256), BF16),
            pltpu.VMEM((9, 256, 128), BF16),
            pltpu.VMEM((9, 128, 256), BF16),
            pltpu.VMEM((ROWS, 128), F32),
            pltpu.VMEM((HALF, 128), F32),
            pltpu.VMEM((plane * CH, 128), BF16),
            pltpu.VMEM((plane - 1, CH, 128), BF16),
            pltpu.VMEM((nhigh, CH, 128), F32),
            dma((6,)),
            dma((4,)), dma((4,)),
            dma, dma,
            dma((plane - 1,)), dma((plane - 1,)),
            dma((nhigh - 1,)), dma((nhigh - 1,)),
            dma((plane - 1,)), dma((plane - 1,)),
            dma, dma,
        ],
        compiler_params=pltpu.CompilerParams(
            collective_id=0, has_side_effects=True, vmem_limit_bytes=48 * 2**20
        ),
    )(
        *[
            pltpu.with_memory_space_constraint(value, pltpu.HBM)
            for value in (
                features, weight_first, weight_second, neighbours, active, cotangent
            )
        ]
    )
    grads = jax.ShapeDtypeStruct((ROWS, C), F32)
    out, gfeat, fa, fb = pl.pallas_call(
        finish,
        out_shape=(brick, brick, grads, grads),
        in_specs=[vmem] * 3,
        out_specs=(hbm,) * 4,
        scratch_shapes=[pltpu.VMEM((ROWS, C), F32), pltpu.VMEM((ROWS, C), F32), dma((4,))],
        compiler_params=pltpu.CompilerParams(vmem_limit_bytes=24 * 2**20),
    )(out, gfeat, full)
    return out, gfeat, fa.reshape(3, 3, 3, C, C), fb.reshape(3, 3, 3, C, C)


def solution(mesh):
    count = mesh.shape["dom"]
    return jax.shard_map(
        functools.partial(on_device, count // (NZ * NCORE), NZ),
        mesh=mesh,
        in_specs=(
            P(("scene", "dom"), None, None, None),
            P(),
            P(),
            P(("scene", "dom"), None),
            P(("scene", "dom")),
            P(("scene", "dom"), None, None, None),
        ),
        out_specs=(
            P(("scene", "dom"), None, None, None),
            P(("scene", "dom"), None, None, None),
            P("scene", None, None, None, None),
            P("scene", None, None, None, None),
        ),
        check_vma=False,
    )
```

time: 66 us -> 50.4 us (0.76)
  Pallas kernels: 57.4 us -> 49.6 us
  local copies, waits for them, and re-layouts: 7.63 us -> 0 us
    pallas_call x1 -> x2, Pallas kernels: 57.4 us -> 49.6 us  [the longest x1 48.2 us: on_device(): pl.pallas_call(functools.partial(kernel, ny, nz, scale), out_shape=(brick...]
    unnamed x16 -> x0, local copies, waits for them, and re-layouts: 7.63 us -> none
where the time goes in v2:
time: 50.4 us; the launch traced here: 50.2 us
  Pallas kernels  49.6 us (98%)
  between operations  0.64 us (1%)
    pallas_call x1, Pallas kernels, on_device(): pl.pallas_call(functools.partial(kernel, ny, nz, scale), out_shape=(brick...  48.2 us
    pallas_call x1, Pallas kernels, on_device(): pl.pallas_call(finish, out_shape=(brick, brick, grads, grads), in_specs=[...  1.37 us

profile of v2, /device:TPU:1, one launch (start us, length us, event | category | flops | bytes accessed | tf_op | source)
XLA Modules:
  0.0 50.2 jit_solution(17946225353174617315)
XLA Ops:
  0.6 48.2 %shard_map.93 = (bf16[2,8,8,512]{3,2,1,0:T(8,128)(2,1)S(1)}, bf16[2,8,8,512]{3,2,1,0:T(8,128)(2,1)S(1)}, bf16[2,16,64,128]{3,2,1,0:T(8,128)(2,1)S(1)}) custom-call(bf16[2,8,8,512]{3,2,1,0:T(8,128)(2,1)} %feat_in.1, bf16[3,3,3,64,64]{4,3,2,1,0:T(8,128)(2,1)} %wa_in.1, bf16[3,3,3,64,64]{4,3,2,1,0:T(8,128)(2,1)} %wb_in.1, s32[2,26]{1,0:T(2,128)} %nb_in.1, ...), custom_call_target="tpu_custom_call" | custom-call | tf_op jit(solution)/shard_map/pallas_call | solution.py:447
  48.9 1.4 %shard_map.94 = (bf16[2,8,8,512]{3,2,1,0:T(8,128)(2,1)}, bf16[2,8,8,512]{3,2,1,0:T(8,128)(2,1)}, f32[1728,64]{1,0:T(8,128)}, f32[1728,64]{1,0:T(8,128)}) custom-call(bf16[2,8,8,512]{3,2,1,0:T(8,128)(2,1)S(1)} %get-tuple-element.11.out_in, bf16[2,8,8,512]{3,2,1,0:T(8,128)(2,1)S(1)} %get-tuple-element.12.gfeat_in, ...), custom_call_target="tpu_custom_call" | custom-call | tf_op jit(solution)/shard_map/pallas_call | solution.py:492

commit v3 on v2

v3 whole, which is shorter than its diff:
```python
import functools
import math

import jax
import jax.numpy as jnp
from jax import lax
from jax.experimental import pallas as pl
from jax.experimental.pallas import tpu as pltpu
from jax.sharding import PartitionSpec as P

C = 64
E = 8
FEAT, GOUT = 0, 1
MID, GHID = 0, 1
TN = (((0,), (0,)), ((), ()))
NT = (((1,), (1,)), ((), ()))
ROWS = 27 * C
HALF = ROWS // 2
NCORE = 2
NZ = 16
ZLOW = 4
CH = 64
F32 = jnp.float32
BF16 = jnp.bfloat16


def entry(nb, brick, offset):
    if offset == (0, 0, 0):
        return 8 * brick
    place = (offset[0] + 1) * 9 + (offset[1] + 1) * 3 + offset[2] + 1
    ident = nb[brick, place if place < 13 else place - 1]
    return jnp.where(ident < 0, -1000, (ident & 1) * 8)


def build_selection(nb, sel, sel_edge):
    row = lax.broadcasted_iota(jnp.int32, (16, 128), 0)
    lane = lax.broadcasted_iota(jnp.int32, (16, 128), 1)
    y = row & 7
    second = row >= 8
    for iz in range(3):
        for c in range(3):
            yy = y + (c - 1)
            wrap = (yy < 0) | (yy > 7)
            for ix in range(3):
                codes = []
                for brick in range(2):
                    inner = entry(nb, brick, (ix - 1, 0, iz - 1))
                    if c == 1:
                        codes.append(jnp.full((16, 128), inner, jnp.int32))
                    else:
                        outer = entry(nb, brick, (ix - 1, c - 1, iz - 1))
                        codes.append(jnp.where(wrap, outer, inner))
                target = jnp.where(second, codes[1], codes[0]) + (yy & 7)
                if ix == 1:
                    for x in range(8):
                        hit = jnp.where(lane == target + 16 * x, 1.0, 0.0).astype(BF16)
                        sel[iz, 128 * c + 16 * x : 128 * c + 16 * x + 16, :] = hit
                else:
                    side = ix // 2
                    hit = jnp.where(lane == target + 16 * side, 1.0, 0.0).astype(BF16)
                    sel_edge[iz, 32 * c + 16 * side : 32 * c + 16 * side + 16, :] = hit[:, :32]


def build_bands(weight, band, band_t):
    zero = jnp.zeros((C, C), BF16)
    for t in range(9):
        taps = [weight[t // 3, t % 3, e] for e in range(3)]
        for zi in range(4):
            left = taps[zi] if zi < 3 else zero
            right = taps[zi - 1] if zi > 0 else zero
            band[t, C * zi : C * zi + C, :] = jnp.concatenate([left, right], axis=1)
        band_t[8 - t, :C, :] = jnp.concatenate([taps[2], taps[1], taps[0], zero], axis=1)
        band_t[8 - t, C:, :] = jnp.concatenate([zero, taps[2], taps[1], taps[0]], axis=1)


def select(source, choose):
    rows = choose.shape[1]
    low = lax.broadcasted_iota(jnp.int32, (rows, 128), 1) < C
    source = pltpu.roll(source.astype(F32), C, 1).astype(BF16)
    edge = source[:, :128]
    inner = jnp.dot(choose[1], source, preferred_element_type=F32)
    before = jnp.dot(choose[0], edge, preferred_element_type=F32)
    after = jnp.dot(choose[2], edge, preferred_element_type=F32)
    first = jnp.where(low, before, inner[:, :128])
    last = jnp.where(low, inner[:, :128], after)
    return jnp.concatenate([first, inner[:, 128:], last], axis=1).astype(BF16)


def pad_inner(layers, sel, padded, field):
    value = select(layers.reshape(128, 512), sel)
    for c in range(3):
        start = 160 * c + 16
        padded[field, start : start + 128, :] = value[128 * c : 128 * c + 128]


def pad_edge(below, above, sel_edge, padded, field):
    value = select(jnp.concatenate([below, above], axis=0), sel_edge)
    for c in range(3):
        padded[field, 160 * c : 160 * c + 16, :] = value[32 * c : 32 * c + 16]
        padded[field, 160 * c + 144 : 160 * c + 160, :] = value[32 * c + 16 : 32 * c + 32]


def multiply(part, tap, flipped):
    if flipped:
        return lax.dot_general(part, tap, NT, preferred_element_type=F32)
    return jnp.dot(part, tap, preferred_element_type=F32)


def convolve(padded, field, band, pair, flipped):
    total = None
    for t in range(9):
        start = 160 * (t % 3) + 16 * (t // 3)
        part = padded[field, start : start + 128, 128 * pair : 128 * pair + 256]
        term = multiply(part, band[t], flipped)
        total = term if total is None else total + term
    return total


def filter_taps(t, late, padded, sums):
    low = lax.broadcasted_iota(jnp.int32, (C, 128), 1) < C
    one = None
    two = None
    at_one = pl.multiple_of(160 * (t % 3) + 16 * (t // 3), 16)
    back = 8 - t
    at_two = pl.multiple_of(160 * (back % 3) + 16 * (back // 3), 16)
    for pair in range(4):
        lanes = slice(128 * pair, 128 * pair + 128)
        wide = slice(128 * pair, 128 * pair + 256)
        ghid = late[GHID, 1:9, :, lanes].reshape(128, 128)
        middle = late[MID, 1:9, :, lanes].reshape(128, 128)
        term = lax.dot_general(
            padded[FEAT, pl.ds(at_one, 128), wide], ghid, TN, preferred_element_type=F32
        )
        one = term if one is None else one + term
        term = lax.dot_general(
            middle, padded[GOUT, pl.ds(at_two, 128), wide], TN, preferred_element_type=F32
        )
        two = term if two is None else two + term
    for e in range(3):
        near = one[C * e : C * e + C]
        far = one[C * e + C : C * e + 2 * C]
        pieces = []
        for value, block in ((two[:C], 2 - e), (two[C:], 3 - e)):
            tile = value[:, 128 * (block // 2) : 128 * (block // 2) + 128]
            pieces.append(tile if block % 2 else pltpu.roll(tile, C, 1))
        first_part = near + pltpu.roll(far, C, 1)
        second_part = pieces[0] + pieces[1]
        start = pl.multiple_of(192 * t + C * e, C)
        sums[pl.ds(start, C), :] = jnp.where(low, first_part, second_part)


def halo_copies(layers, send, recv, count, me):
    up = (me + 1) % count
    down = (me + count - 1) % count
    return [
        pltpu.make_async_remote_copy(
            src_ref=layers.at[:, source],
            dst_ref=layers.at[:, target],
            send_sem=send.at[way],
            recv_sem=recv.at[way],
            device_id={"dom": device},
        )
        for way, (source, target, device) in enumerate(((8, 0, up), (1, 9, down)))
    ]


def halo_start(copies, count, me):
    @pl.when(me < count - 1)
    def _():
        copies[0].start()

    @pl.when(me > 0)
    def _():
        copies[1].start()


def halo_wait(copies, count, me):
    @pl.when(me < count - 1)
    def _():
        copies[0].wait_send()
        copies[1].wait_recv()

    @pl.when(me > 0)
    def _():
        copies[1].wait_send()
        copies[0].wait_recv()


def prepare(
    count,
    feat_in, wa_in, wb_in, nb_in, act_in, cot_in,
    given, padded, sel, sel_edge, band_a, band_at, band_b, band_bt, alive,
    feat, cot, wa, wb, nb, act, raw,
    in_sem, halo_send, halo_recv,
):
    me = lax.axis_index("dom")
    raw[:, 0] = jnp.zeros((2, 16, 512), BF16)
    raw[:, 9] = jnp.zeros((2, 16, 512), BF16)
    barrier = pltpu.get_barrier_semaphore()
    pl.semaphore_signal(barrier, inc=1, device_id={"dom": (me + 1) % count})
    pl.semaphore_signal(barrier, inc=1, device_id={"dom": (me + count - 1) % count})
    loads = [
        pltpu.make_async_copy(source, target, in_sem.at[i])
        for i, (source, target) in enumerate(
            ((act_in, act), (feat_in, feat), (cot_in, cot), (nb_in, nb), (wa_in, wa), (wb_in, wb))
        )
    ]
    for load in loads:
        load.start()
    for load in loads[:3]:
        load.wait()
    keep = [jnp.where(act[b] > 0, 1.0, 0.0) for b in range(2)]
    raw[FEAT, 1:9] = jnp.concatenate(
        [feat[b].astype(F32) for b in range(2)], axis=1
    ).astype(BF16)
    raw[GOUT, 1:9] = jnp.concatenate(
        [cot[b].astype(F32) * keep[b] for b in range(2)], axis=1
    ).astype(BF16)
    pl.semaphore_wait(barrier, 2)
    halo = halo_copies(raw, halo_send, halo_recv, count, me)
    halo_start(halo, count, me)
    given[...] = raw[:, 1:9]
    rows = lax.broadcasted_iota(jnp.int32, (128, 128), 0)
    alive[...] = jnp.where((rows & 8) == 0, keep[0], keep[1])
    for load in loads[3:]:
        load.wait()
    build_selection(nb, sel, sel_edge)
    for field in (FEAT, GOUT):
        pad_inner(raw[field, 1:9], sel, padded, field)
    build_bands(wa, band_a, band_at)
    build_bands(wb, band_b, band_bt)
    halo_wait(halo, count, me)
    for field in (FEAT, GOUT):
        pad_edge(raw[field, 0], raw[field, 9], sel_edge, padded, field)


def kernel(
    ny, nz, scale,
    given, padded, sel, sel_edge, band_a, band_at, band_b, band_bt, alive,
    out, gfeat, full,
    late, late_padded, sums, from_core, chip, from_plane, groups,
    halo_send, halo_recv, core_send, core_recv, plane_send, plane_recv,
    group_send, group_recv, back_send, back_recv, last_send, last_recv,
):
    count = ny * nz * NCORE
    plane = ny * ZLOW
    nhigh = nz // ZLOW
    live = -(-HALF // CH)
    me = lax.axis_index("dom")
    core = me % NCORE
    y = me // (NCORE * nz)
    shift = (ZLOW // 2) * core
    z = ((me // NCORE) % nz + shift) % nz
    zlow = z % ZLOW
    zhigh = z // ZLOW
    spot = y * ZLOW + zlow
    partner = me + 1 - 2 * core
    order = sorted(
        range(1, plane),
        key=lambda step: (0, 1, 2, 1)[step // ZLOW] + (0, 1, 2, 2)[step % ZLOW],
        reverse=True,
    )

    def device_at(ty, tz):
        return (ty * nz + (tz + nz - shift) % nz) * NCORE + core

    def at_plane(step):
        return device_at((spot ^ step) // ZLOW, zhigh * ZLOW + (spot ^ step) % ZLOW)

    def at_group(step):
        return device_at(y, ((zhigh + step) % nhigh) * ZLOW + zlow)

    late[:, 0] = jnp.zeros((2, 16, 512), BF16)
    late[:, 9] = jnp.zeros((2, 16, 512), BF16)
    barrier = pltpu.get_barrier_semaphore()
    for step in range(1, nhigh):
        pl.semaphore_signal(barrier, inc=1, device_id={"dom": at_group(step)})
    for step in order:
        pl.semaphore_signal(barrier, inc=1, device_id={"dom": at_plane(step)})
    pl.semaphore_signal(barrier, inc=1, device_id={"dom": (me + 1) % count})
    pl.semaphore_signal(barrier, inc=1, device_id={"dom": (me + count - 1) % count})

    chip[HALF:, :] = jnp.zeros((CH * plane - HALF, 128), BF16)
    for pair in range(4):
        lanes = slice(128 * pair, 128 * pair + 128)
        h = convolve(padded, FEAT, band_a, pair, False)
        g = convolve(padded, GOUT, band_bt, pair, True)
        s = jax.nn.sigmoid(h)
        middle = alive[...] * (h * s)
        ghid = g * (s * (1.0 + h * (1.0 - s)))
        late[MID, 1:9, :, lanes] = middle.astype(BF16).reshape(8, 16, 128)
        late[GHID, 1:9, :, lanes] = ghid.astype(BF16).reshape(8, 16, 128)
    for i in range(5):
        filter_taps(4 * (1 - core) + i, late, padded, sums)
    pl.semaphore_wait(barrier, 2 + plane - 1 + nhigh - 1)

    own = pl.multiple_of(core * HALF, 8)
    other = pl.multiple_of((1 - core) * HALF, 8)
    to_core = pltpu.make_async_remote_copy(
        src_ref=sums.at[pl.ds(other, HALF)],
        dst_ref=from_core,
        send_sem=core_send,
        recv_sem=core_recv,
        device_id={"dom": partner},
    )
    to_core.start()
    halo = halo_copies(late, halo_send, halo_recv, count, me)
    halo_start(halo, count, me)
    for i in range(4):
        filter_taps(5 * core + i, late, padded, sums)
    to_core.wait_recv()
    from_core[...] = from_core[...] + sums[pl.ds(own, HALF), :]
    chip[:HALF, :] = from_core[...].astype(BF16)

    def plane_copy(step):
        return pltpu.make_async_remote_copy(
            src_ref=chip.at[pl.ds(pl.multiple_of((spot ^ step) * CH, CH), CH)],
            dst_ref=from_plane.at[step - 1],
            send_sem=plane_send.at[step - 1],
            recv_sem=plane_recv.at[step - 1],
            device_id={"dom": at_plane(step)},
        )

    for step in order:

        @pl.when((spot ^ step) < live)
        def _():
            plane_copy(step).start()

    def last(field, band, flipped, target, base):
        for pair in range(4):
            lanes = slice(128 * pair, 128 * pair + 128)
            value = convolve(late_padded, field, band, pair, flipped)
            if flipped:
                value = value * alive[...]
            value = value.reshape(8, 16, 128) + given[base, :, :, lanes].astype(F32)
            for b in range(2):
                target[b, :, :, lanes] = value[:, 8 * b : 8 * b + 8].astype(BF16)

    halo_wait(halo, count, me)
    for field in (MID, GHID):
        pad_inner(late[field, 1:9], sel, late_padded, field)
        pad_edge(late[field, 0], late[field, 9], sel_edge, late_padded, field)
    last(MID, band_b, False, out, FEAT)

    to_group = [
        pltpu.make_async_remote_copy(
            src_ref=groups.at[zhigh],
            dst_ref=groups.at[zhigh],
            send_sem=group_send.at[step - 1],
            recv_sem=group_recv.at[step - 1],
            device_id={"dom": at_group(step)},
        )
        for step in range(1, nhigh)
    ]
    back = {
        step: pltpu.make_async_remote_copy(
            src_ref=full.at[core, spot],
            dst_ref=full.at[core, spot],
            send_sem=back_send.at[step - 1],
            recv_sem=back_recv.at[step - 1],
            device_id={"dom": at_plane(step)},
        )
        for step in order
    }

    def forward(place):
        return pltpu.make_async_remote_copy(
            src_ref=full.at[core, place],
            dst_ref=full.at[core, place],
            send_sem=last_send.at[place],
            recv_sem=last_recv.at[place],
            device_id={"dom": partner},
        )

    @pl.when(spot < live)
    def _():
        total = chip[pl.ds(pl.multiple_of(spot * CH, CH), CH), :].astype(F32)
        for step in order:
            plane_copy(step).wait_recv()
        for step in range(1, plane):
            total = total + from_plane[step - 1].astype(F32)
        groups[zhigh] = total.astype(BF16)
        for copy in to_group:
            copy.start()

    last(GHID, band_at, True, gfeat, GOUT)

    @pl.when(spot < live)
    def _():
        for copy in to_group:
            copy.wait_recv()
        total = groups[0].astype(F32)
        for i in range(1, nhigh):
            total = total + groups[i].astype(F32)
        full[core, spot] = (total * scale).astype(BF16)
        for step in order:
            back[step].start()
        forward(spot).start()

    to_core.wait_send()
    for step in order:

        @pl.when((spot ^ step) < live)
        def _():
            plane_copy(step).wait_send()

    for step in order[::-1]:

        @pl.when((spot ^ step) < live)
        def _():
            back[step].wait_recv()
            forward(spot ^ step).start()

    @pl.when(spot < live)
    def _():
        for copy in to_group:
            copy.wait_send()
        for step in order:
            back[step].wait_send()

    for place in range(live):
        forward(place).wait()


def finish(out_in, gfeat_in, full, out, gfeat, fa, fb, fa_here, fb_here, sems):
    copies = [
        pltpu.make_async_copy(out_in, out, sems.at[0]),
        pltpu.make_async_copy(gfeat_in, gfeat, sems.at[1]),
    ]
    for copy in copies:
        copy.start()
    for h in range(NCORE):
        rows = slice(h * HALF, h * HALF + HALF)
        value = full[h].reshape(full.shape[1] * CH, 128)[:HALF].astype(F32)
        fa_here[rows, :] = value[:, :C]
        fb_here[rows, :] = pltpu.roll(value, C, 1)[:, :C]
        for i, (here, there) in enumerate(((fa_here, fa), (fb_here, fb))):
            copy = pltpu.make_async_copy(here.at[rows], there.at[rows], sems.at[2 + 2 * h + i])
            copy.start()
            copies.append(copy)
    for copy in copies:
        copy.wait()


def on_device(ny, nz, features, weight_first, weight_second, neighbours, active, cotangent):
    count = ny * nz * NCORE
    scale = 1.0 / math.sqrt(2 * count * E**3)
    plane = ny * ZLOW
    nhigh = nz // ZLOW
    vmem = pl.BlockSpec(memory_space=pltpu.VMEM)
    hbm = pl.BlockSpec(memory_space=pltpu.HBM)
    dma = pltpu.SemaphoreType.DMA
    brick = jax.ShapeDtypeStruct(features.shape, BF16)
    whole = pltpu.VMEM(features.shape, BF16)
    taps = pltpu.VMEM(weight_first.shape, BF16)
    prepared = pl.pallas_call(
        functools.partial(prepare, count),
        out_shape=(
            jax.ShapeDtypeStruct((2, 8, 16, 512), BF16),
            jax.ShapeDtypeStruct((2, 480, 640), BF16),
            jax.ShapeDtypeStruct((3, 384, 128), BF16),
            jax.ShapeDtypeStruct((3, 96, 32), BF16),
            jax.ShapeDtypeStruct((9, 256, 128), BF16),
            jax.ShapeDtypeStruct((9, 128, 256), BF16),
            jax.ShapeDtypeStruct((9, 256, 128), BF16),
            jax.ShapeDtypeStruct((9, 128, 256), BF16),
            jax.ShapeDtypeStruct((128, 128), F32),
        ),
        in_specs=[hbm] * 6,
        out_specs=(vmem,) * 9,
        scratch_shapes=[
            whole, whole, taps, taps,
            pltpu.SMEM(neighbours.shape, jnp.int32),
            pltpu.SMEM(active.shape, jnp.int32),
            pltpu.VMEM((2, 10, 16, 512), BF16),
            dma((6,)), dma((2,)), dma((2,)),
        ],
        compiler_params=pltpu.CompilerParams(
            collective_id=0, has_side_effects=True, vmem_limit_bytes=24 * 2**20
        ),
    )(
        *[
            pltpu.with_memory_space_constraint(value, pltpu.HBM)
            for value in (
                features, weight_first, weight_second, neighbours, active, cotangent
            )
        ]
    )
    out, gfeat, full = pl.pallas_call(
        functools.partial(kernel, ny, nz, scale),
        out_shape=(brick, brick, jax.ShapeDtypeStruct((NCORE, plane, CH, 128), BF16)),
        in_specs=[vmem] * 9,
        out_specs=(vmem, vmem, vmem),
        scratch_shapes=[
            pltpu.VMEM((2, 10, 16, 512), BF16),
            pltpu.VMEM((2, 480, 640), BF16),
            pltpu.VMEM((ROWS, 128), F32),
            pltpu.VMEM((HALF, 128), F32),
            pltpu.VMEM((plane * CH, 128), BF16),
            pltpu.VMEM((plane - 1, CH, 128), BF16),
            pltpu.VMEM((nhigh, CH, 128), BF16),
            dma((2,)), dma((2,)),
            dma, dma,
            dma((plane - 1,)), dma((plane - 1,)),
            dma((nhigh - 1,)), dma((nhigh - 1,)),
            dma((plane - 1,)), dma((plane - 1,)),
            dma((plane,)), dma((plane,)),
        ],
        compiler_params=pltpu.CompilerParams(
            collective_id=1, has_side_effects=True, vmem_limit_bytes=24 * 2**20
        ),
    )(*prepared)
    grads = jax.ShapeDtypeStruct((ROWS, C), F32)
    out, gfeat, fa, fb = pl.pallas_call(
        finish,
        out_shape=(brick, brick, grads, grads),
        in_specs=[vmem] * 3,
        out_specs=(hbm,) * 4,
        scratch_shapes=[pltpu.VMEM((ROWS, C), F32), pltpu.VMEM((ROWS, C), F32), dma((6,))],
        compiler_params=pltpu.CompilerParams(vmem_limit_bytes=24 * 2**20),
    )(out, gfeat, full)
    return out, gfeat, fa.reshape(3, 3, 3, C, C), fb.reshape(3, 3, 3, C, C)


def solution(mesh):
    count = mesh.shape["dom"]
    return jax.shard_map(
        functools.partial(on_device, count // (NZ * NCORE), NZ),
        mesh=mesh,
        in_specs=(
            P(("scene", "dom"), None, None, None),
            P(),
            P(),
            P(("scene", "dom"), None),
            P(("scene", "dom")),
            P(("scene", "dom"), None, None, None),
        ),
        out_specs=(
            P(("scene", "dom"), None, None, None),
            P(("scene", "dom"), None, None, None),
            P("scene", None, None, None, None),
            P("scene", None, None, None, None),
        ),
        check_vma=False,
    )
```

time: 50.4 us -> 46.4 us (0.921)
  Pallas kernels: 49.6 us -> 45.6 us
    pallas_call x1, Pallas kernels: 48.2 us -> 29.6 us  [on_device(): pl.pallas_call(functools.partial(kernel, ny, nz, scale), out_shape=(brick...]
    pallas_call x0 -> x1, Pallas kernels: none -> 14.7 us  [on_device(): pl.pallas_call(functools.partial(prepare, count), out_shape=(jax.ShapeDty...]
where the time goes in v3:
time: 46.4 us; the launch traced here: 46.2 us
  Pallas kernels  45.6 us (98%)
  between operations  0.65 us (1%)
    pallas_call x1, Pallas kernels, on_device(): pl.pallas_call(functools.partial(kernel, ny, nz, scale), out_shape=(brick...  29.6 us
    pallas_call x1, Pallas kernels, on_device(): pl.pallas_call(functools.partial(prepare, count), out_shape=(jax.ShapeDty...  14.7 us
    pallas_call x1, Pallas kernels, on_device(): pl.pallas_call(finish, out_shape=(brick, brick, grads, grads), in_specs=[...  1.34 us

profile of v3, /device:TPU:1, one launch (start us, length us, event | category | flops | bytes accessed | tf_op | source)
XLA Modules:
  0.0 46.2 jit_solution(16831815566029901)
XLA Ops:
  0.6 14.7 %shard_map.93 = (bf16[2,8,16,512]{3,2,1,0:T(8,128)(2,1)S(1)}, bf16[2,480,640]{2,1,0:T(8,128)(2,1)S(1)}, bf16[3,384,128]{2,1,0:T(8,128)(2,1)S(1)}, bf16[3,96,32]{...) custom-call(bf16[2,8,8,512]{3,2,1,0:T(8,128)(2,1)} %feat_in.1, ...), custom_call_target="tpu_custom_call" | custom-call | tf_op jit(solution)/shard_map/pallas_call | solution.py:457
  15.3 29.6 %shard_map.94 = (bf16[2,8,8,512]{3,2,1,0:T(8,128)(2,1)S(1)}, bf16[2,8,8,512]{3,2,1,0:T(8,128)(2,1)S(1)}, bf16[2,16,64,128]{3,2,1,0:T(8,128)(2,1)S(1)}) custom-call(bf16[2,8,16,512]{3,2,1,0:T(8,128)(2,1)S(1)} %get-tuple-element.20.given, bf16[2,480,640]{2,1,0:T(8,128)(2,1)S(1)} %get-tuple-element.21.padded, bf16[3,384,128]{2,1,0:T(8,128)(2,1)S(1)} %get-tuple-element.22.sel, ...), custom_call_target="tpu_custom_call" | custom-call | tf_op jit(solution)/shard_map/pallas_call | solution.py:490
  44.9 1.3 %shard_map.95 = (bf16[2,8,8,512]{3,2,1,0:T(8,128)(2,1)}, bf16[2,8,8,512]{3,2,1,0:T(8,128)(2,1)}, f32[1728,64]{1,0:T(8,128)}, f32[1728,64]{1,0:T(8,128)}) custom-call(bf16[2,8,8,512]{3,2,1,0:T(8,128)(2,1)S(1)} %get-tuple-element.29.out_in, bf16[2,8,8,512]{3,2,1,0:T(8,128)(2,1)S(1)} %get-tuple-element.30.gfeat_in, ...), custom_call_target="tpu_custom_call" | custom-call | tf_op jit(solution)/shard_map/pallas_call | solution.py:515

commit v4 on v3

--- a/solution.py
+++ b/solution.py
@@ -149,53 +149,57 @@
         sums[pl.ds(start, C), :] = jnp.where(low, first_part, second_part)
 
 
-def halo_copies(layers, send, recv, count, me):
-    up = (me + 1) % count
-    down = (me + count - 1) % count
+def halo_copies(places, send, recv, count, me):
+    devices = ((me + 1) % count, (me + count - 1) % count)
     return [
         pltpu.make_async_remote_copy(
-            src_ref=layers.at[:, source],
-            dst_ref=layers.at[:, target],
-            send_sem=send.at[way],
-            recv_sem=recv.at[way],
-            device_id={"dom": device},
-        )
-        for way, (source, target, device) in enumerate(((8, 0, up), (1, 9, down)))
+            src_ref=source,
+            dst_ref=target,
+            send_sem=send.at[i],
+            recv_sem=recv.at[i],
+            device_id={"dom": devices[i % 2]},
+        )
+        for i, (source, target) in enumerate(places)
     ]
 
 
 def halo_start(copies, count, me):
     @pl.when(me < count - 1)
     def _():
-        copies[0].start()
+        for copy in copies[::2]:
+            copy.start()
 
     @pl.when(me > 0)
     def _():
-        copies[1].start()
+        for copy in copies[1::2]:
+            copy.start()
 
 
 def halo_wait(copies, count, me):
     @pl.when(me < count - 1)
     def _():
-        copies[0].wait_send()
-        copies[1].wait_recv()
+        for copy in copies[::2]:
+            copy.wait_send()
+        for copy in copies[1::2]:
+            copy.wait_recv()
 
     @pl.when(me > 0)
     def _():
-        copies[1].wait_send()
-        copies[0].wait_recv()
+        for copy in copies[1::2]:
+            copy.wait_send()
+        for copy in copies[::2]:
+            copy.wait_recv()
 
 
 def prepare(
     count,
     feat_in, wa_in, wb_in, nb_in, act_in, cot_in,
     given, padded, sel, sel_edge, band_a, band_at, band_b, band_bt, alive,
-    feat, cot, wa, wb, nb, act, raw,
+    feat, cot, wa, wb, nb, act, edge,
     in_sem, halo_send, halo_recv,
 ):
     me = lax.axis_index("dom")
-    raw[:, 0] = jnp.zeros((2, 16, 512), BF16)
-    raw[:, 9] = jnp.zeros((2, 16, 512), BF16)
+    edge[...] = jnp.zeros(edge.shape, BF16)
     barrier = pltpu.get_barrier_semaphore()
     pl.semaphore_signal(barrier, inc=1, device_id={"dom": (me + 1) % count})
     pl.semaphore_signal(barrier, inc=1, device_id={"dom": (me + count - 1) % count})
@@ -207,31 +211,35 @@
     ]
     for load in loads:
         load.start()
-    for load in loads[:3]:
+    pl.semaphore_wait(barrier, 2)
+    places = []
+    for field, values in ((FEAT, feat_in), (GOUT, cot_in)):
+        places.append((values.at[:, E - 1], edge.at[field, 0]))
+        places.append((values.at[:, 0], edge.at[field, 1]))
+    halo = halo_copies(places, halo_send, halo_recv, count, me)
+    halo_start(halo, count, me)
+    for load in loads[:4]:
         load.wait()
     keep = [jnp.where(act[b] > 0, 1.0, 0.0) for b in range(2)]
-    raw[FEAT, 1:9] = jnp.concatenate(
-        [feat[b].astype(F32) for b in range(2)], axis=1
-    ).astype(BF16)
-    raw[GOUT, 1:9] = jnp.concatenate(
+    given[FEAT] = jnp.concatenate([feat[b].astype(F32) for b in range(2)], axis=1).astype(BF16)
+    given[GOUT] = jnp.concatenate(
         [cot[b].astype(F32) * keep[b] for b in range(2)], axis=1
     ).astype(BF16)
-    pl.semaphore_wait(barrier, 2)
-    halo = halo_copies(raw, halo_send, halo_recv, count, me)
-    halo_start(halo, count, me)
-    given[...] = raw[:, 1:9]
     rows = lax.broadcasted_iota(jnp.int32, (128, 128), 0)
     alive[...] = jnp.where((rows & 8) == 0, keep[0], keep[1])
-    for load in loads[3:]:
-        load.wait()
     build_selection(nb, sel, sel_edge)
     for field in (FEAT, GOUT):
-        pad_inner(raw[field, 1:9], sel, padded, field)
+        pad_inner(given[field], sel, padded, field)
+    for load in loads[4:]:
+        load.wait()
     build_bands(wa, band_a, band_at)
     build_bands(wb, band_b, band_bt)
     halo_wait(halo, count, me)
     for field in (FEAT, GOUT):
-        pad_edge(raw[field, 0], raw[field, 9], sel_edge, padded, field)
+        below, above = [
+            edge[field, side].astype(F32).reshape(16, 512).astype(BF16) for side in range(2)
+        ]
+        pad_edge(below, above, sel_edge, padded, field)
 
 
 def kernel(
@@ -240,7 +248,7 @@
     out, gfeat, full,
     late, late_padded, sums, from_core, chip, from_plane, groups,
     halo_send, halo_recv, core_send, core_recv, plane_send, plane_recv,
-    group_send, group_recv, back_send, back_recv, last_send, last_recv,
+    group_send, group_recv, back_send, back_recv, last_send, last_recv, relay,
 ):
     count = ny * nz * NCORE
     plane = ny * ZLOW
@@ -249,36 +257,46 @@
     me = lax.axis_index("dom")
     core = me % NCORE
     y = me // (NCORE * nz)
-    shift = (ZLOW // 2) * core
-    z = ((me // NCORE) % nz + shift) % nz
+    z = (me // NCORE) % nz
     zlow = z % ZLOW
     zhigh = z // ZLOW
     spot = y * ZLOW + zlow
     partner = me + 1 - 2 * core
+    steps = [(dy, dz) for dy in range(ny) for dz in range(ZLOW) if dy or dz]
     order = sorted(
-        range(1, plane),
-        key=lambda step: (0, 1, 2, 1)[step // ZLOW] + (0, 1, 2, 2)[step % ZLOW],
+        range(len(steps)),
+        key=lambda i: (0, 1, 2, 1)[steps[i][0]] + (0, 1, 1, 2)[steps[i][1]],
         reverse=True,
     )
 
-    def device_at(ty, tz):
-        return (ty * nz + (tz + nz - shift) % nz) * NCORE + core
-
-    def at_plane(step):
-        return device_at((spot ^ step) // ZLOW, zhigh * ZLOW + (spot ^ step) % ZLOW)
+    def ahead(i):
+        dy, dz = steps[i]
+        return y ^ dy, (z + nz + (0, 1, -1, 2 - 4 * core)[dz]) % nz
+
+    def behind(i):
+        dy, dz = steps[i]
+        return y ^ dy, (z + nz - (0, 1, -1, 2 - 4 * core)[dz]) % nz
+
+    def device_at(place):
+        return (place[0] * nz + place[1]) * NCORE + core
+
+    def spot_at(place):
+        return place[0] * ZLOW + place[1] % ZLOW
 
     def at_group(step):
-        return device_at(y, ((zhigh + step) % nhigh) * ZLOW + zlow)
-
+        return device_at((y, (z + step * ZLOW) % nz))
+
+    near = sorted({1, nhigh - 1})
+    far = nhigh > 3
+    greeted = [device_at(ahead(i)) for i in order]
+    greeted += [device_at(behind(i)) for i in order if steps[i][1] == 3]
+    greeted += [at_group(step) for step in (near if far else range(1, nhigh))]
+    greeted += [(me + 1) % count, (me + count - 1) % count]
     late[:, 0] = jnp.zeros((2, 16, 512), BF16)
     late[:, 9] = jnp.zeros((2, 16, 512), BF16)
     barrier = pltpu.get_barrier_semaphore()
-    for step in range(1, nhigh):
-        pl.semaphore_signal(barrier, inc=1, device_id={"dom": at_group(step)})
-    for step in order:
-        pl.semaphore_signal(barrier, inc=1, device_id={"dom": at_plane(step)})
-    pl.semaphore_signal(barrier, inc=1, device_id={"dom": (me + 1) % count})
-    pl.semaphore_signal(barrier, inc=1, device_id={"dom": (me + count - 1) % count})
+    for device in greeted:
+        pl.semaphore_signal(barrier, inc=1, device_id={"dom": device})
 
     chip[HALF:, :] = jnp.zeros((CH * plane - HALF, 128), BF16)
     for pair in range(4):
@@ -292,7 +310,10 @@
         late[GHID, 1:9, :, lanes] = ghid.astype(BF16).reshape(8, 16, 128)
     for i in range(5):
         filter_taps(4 * (1 - core) + i, late, padded, sums)
-    pl.semaphore_wait(barrier, 2 + plane - 1 + nhigh - 1)
+    pl.semaphore_wait(barrier, len(greeted))
+    if far:
+        for step in near:
+            pl.semaphore_signal(relay, inc=1, device_id={"dom": at_group(step)})
 
     own = pl.multiple_of(core * HALF, 8)
     other = pl.multiple_of((1 - core) * HALF, 8)
@@ -304,7 +325,10 @@
         device_id={"dom": partner},
     )
     to_core.start()
-    halo = halo_copies(late, halo_send, halo_recv, count, me)
+    halo = halo_copies(
+        ((late.at[:, E], late.at[:, 0]), (late.at[:, 1], late.at[:, E + 1])),
+        halo_send, halo_recv, count, me,
+    )
     halo_start(halo, count, me)
     for i in range(4):
         filter_taps(5 * core + i, late, padded, sums)
@@ -312,20 +336,21 @@
     from_core[...] = from_core[...] + sums[pl.ds(own, HALF), :]
     chip[:HALF, :] = from_core[...].astype(BF16)
 
-    def plane_copy(step):
+    def plane_copy(i):
+        begin = pl.multiple_of(spot_at(ahead(i)) * CH, CH)
         return pltpu.make_async_remote_copy(
-            src_ref=chip.at[pl.ds(pl.multiple_of((spot ^ step) * CH, CH), CH)],
-            dst_ref=from_plane.at[step - 1],
-            send_sem=plane_send.at[step - 1],
-            recv_sem=plane_recv.at[step - 1],
-            device_id={"dom": at_plane(step)},
-        )
-
-    for step in order:
-
-        @pl.when((spot ^ step) < live)
+            src_ref=chip.at[pl.ds(begin, CH)],
+            dst_ref=from_plane.at[i],
+            send_sem=plane_send.at[i],
+            recv_sem=plane_recv.at[i],
+            device_id={"dom": device_at(ahead(i))},
+        )
+
+    for i in order:
+
+        @pl.when(spot_at(ahead(i)) < live)
         def _():
-            plane_copy(step).start()
+            plane_copy(i).start()
 
     def last(field, band, flipped, target, base):
         for pair in range(4):
@@ -351,18 +376,18 @@
             recv_sem=group_recv.at[step - 1],
             device_id={"dom": at_group(step)},
         )
-        for step in range(1, nhigh)
+        for step in sorted(range(1, nhigh), key=lambda step: -min(step, nhigh - step))
     ]
-    back = {
-        step: pltpu.make_async_remote_copy(
+    back = [
+        pltpu.make_async_remote_copy(
             src_ref=full.at[core, spot],
             dst_ref=full.at[core, spot],
-            send_sem=back_send.at[step - 1],
-            recv_sem=back_recv.at[step - 1],
-            device_id={"dom": at_plane(step)},
-        )
-        for step in order
-    }
+            send_sem=back_send.at[i],
+            recv_sem=back_recv.at[i],
+            device_id={"dom": device_at(behind(i))},
+        )
+        for i in range(len(steps))
+    ]
 
     def forward(place):
         return pltpu.make_async_remote_copy(
@@ -373,13 +398,16 @@
             device_id={"dom": partner},
         )
 
+    if far:
+        pl.semaphore_wait(relay, len(near))
+
     @pl.when(spot < live)
     def _():
         total = chip[pl.ds(pl.multiple_of(spot * CH, CH), CH), :].astype(F32)
-        for step in order:
-            plane_copy(step).wait_recv()
-        for step in range(1, plane):
-            total = total + from_plane[step - 1].astype(F32)
+        for i in order:
+            plane_copy(i).wait_recv()
+        for i in range(len(steps)):
+            total = total + from_plane[i].astype(F32)
         groups[zhigh] = total.astype(BF16)
         for copy in to_group:
             copy.start()
@@ -394,30 +422,30 @@
         for i in range(1, nhigh):
             total = total + groups[i].astype(F32)
         full[core, spot] = (total * scale).astype(BF16)
-        for step in order:
-            back[step].start()
+        for i in order:
+            back[i].start()
         forward(spot).start()
 
     to_core.wait_send()
-    for step in order:
-
-        @pl.when((spot ^ step) < live)
+    for i in order:
+
+        @pl.when(spot_at(ahead(i)) < live)
         def _():
-            plane_copy(step).wait_send()
-
-    for step in order[::-1]:
-
-        @pl.when((spot ^ step) < live)
+            plane_copy(i).wait_send()
+
+    for i in order[::-1]:
+
+        @pl.when(spot_at(ahead(i)) < live)
         def _():
-            back[step].wait_recv()
-            forward(spot ^ step).start()
+            back[i].wait_recv()
+            forward(spot_at(ahead(i))).start()
 
     @pl.when(spot < live)
     def _():
         for copy in to_group:
             copy.wait_send()
-        for step in order:
-            back[step].wait_send()
+        for copy in back:
+            copy.wait_send()
 
     for place in range(live):
         forward(place).wait()
@@ -473,8 +501,8 @@
             whole, whole, taps, taps,
             pltpu.SMEM(neighbours.shape, jnp.int32),
             pltpu.SMEM(active.shape, jnp.int32),
-            pltpu.VMEM((2, 10, 16, 512), BF16),
-            dma((6,)), dma((2,)), dma((2,)),
+            pltpu.VMEM((2, 2, 2, E, 512), BF16),
+            dma((6,)), dma((4,)), dma((4,)),
         ],
         compiler_params=pltpu.CompilerParams(
             collective_id=0, has_side_effects=True, vmem_limit_bytes=24 * 2**20
@@ -506,6 +534,7 @@
             dma((nhigh - 1,)), dma((nhigh - 1,)),
             dma((plane - 1,)), dma((plane - 1,)),
             dma((plane,)), dma((plane,)),
+            pltpu.SemaphoreType.REGULAR,
         ],
         compiler_params=pltpu.CompilerParams(
             collective_id=1, has_side_effects=True, vmem_limit_bytes=24 * 2**20

time: 46.4 us -> 43.9 us (0.946)
  Pallas kernels: 45.6 us -> 43.1 us
    pallas_call x1, Pallas kernels: 29.6 us -> 26.8 us  [on_device(): pl.pallas_call(functools.partial(kernel, ny, nz, scale), out_shape=(brick...]
where the time goes in v4:
time: 43.9 us; the launch traced here: 43.7 us
  Pallas kernels  43.1 us (98%)
  between operations  0.65 us (1%)
    pallas_call x1, Pallas kernels, on_device(): pl.pallas_call(functools.partial(kernel, ny, nz, scale), out_shape=(brick...  26.8 us
    pallas_call x1, Pallas kernels, on_device(): pl.pallas_call(functools.partial(prepare, count), out_shape=(jax.ShapeDty...  14.9 us
    pallas_call x1, Pallas kernels, on_device(): pl.pallas_call(finish, out_shape=(brick, brick, grads, grads), in_specs=[...  1.34 us

profile of v4, /device:TPU:1, one launch (start us, length us, event | category | flops | bytes accessed | tf_op | source)
XLA Modules:
  0.0 43.7 jit_solution(1242686636177967515)
XLA Ops:
  0.6 14.9 %shard_map.93 = (bf16[2,8,16,512]{3,2,1,0:T(8,128)(2,1)S(1)}, bf16[2,480,640]{2,1,0:T(8,128)(2,1)S(1)}, bf16[3,384,128]{2,1,0:T(8,128)(2,1)S(1)}, bf16[3,96,32]{...) custom-call(bf16[2,8,8,512]{3,2,1,0:T(8,128)(2,1)} %feat_in.1, ...), custom_call_target="tpu_custom_call" | custom-call | tf_op jit(solution)/shard_map/pallas_call | solution.py:485
  15.6 26.8 %shard_map.94 = (bf16[2,8,8,512]{3,2,1,0:T(8,128)(2,1)S(1)}, bf16[2,8,8,512]{3,2,1,0:T(8,128)(2,1)S(1)}, bf16[2,16,64,128]{3,2,1,0:T(8,128)(2,1)S(1)}) custom-call(bf16[2,8,16,512]{3,2,1,0:T(8,128)(2,1)S(1)} %get-tuple-element.20.given, bf16[2,480,640]{2,1,0:T(8,128)(2,1)S(1)} %get-tuple-element.21.padded, bf16[3,384,128]{2,1,0:T(8,128)(2,1)S(1)} %get-tuple-element.22.sel, ...), custom_call_target="tpu_custom_call" | custom-call | tf_op jit(solution)/shard_map/pallas_call | solution.py:518
  42.4 1.3 %shard_map.95 = (bf16[2,8,8,512]{3,2,1,0:T(8,128)(2,1)}, bf16[2,8,8,512]{3,2,1,0:T(8,128)(2,1)}, f32[1728,64]{1,0:T(8,128)}, f32[1728,64]{1,0:T(8,128)}) custom-call(bf16[2,8,8,512]{3,2,1,0:T(8,128)(2,1)S(1)} %get-tuple-element.29.out_in, bf16[2,8,8,512]{3,2,1,0:T(8,128)(2,1)S(1)} %get-tuple-element.30.gfeat_in, ...), custom_call_target="tpu_custom_call" | custom-call | tf_op jit(solution)/shard_map/pallas_call | solution.py:544

commit v5 on v4

--- a/solution.py
+++ b/solution.py
@@ -116,6 +116,25 @@
     return total
 
 
+def convolve_edge(padded, field, band, flipped):
+    sides = []
+    for layer, a in ((0, 0), (9, 2)):
+        total = None
+        for c in range(3):
+            start = 160 * c + 16 * layer
+            part = jnp.concatenate(
+                [
+                    padded[field, start : start + 16, 128 * pair : 128 * pair + 256]
+                    for pair in range(4)
+                ],
+                axis=0,
+            )
+            term = multiply(part, band[3 * a + c], flipped)
+            total = term if total is None else total + term
+        sides.append(total)
+    return sides
+
+
 def filter_taps(t, late, padded, sums):
     low = lax.broadcasted_iota(jnp.int32, (C, 128), 1) < C
     one = None
@@ -191,62 +210,14 @@
             copy.wait_recv()
 
 
-def prepare(
-    count,
-    feat_in, wa_in, wb_in, nb_in, act_in, cot_in,
-    given, padded, sel, sel_edge, band_a, band_at, band_b, band_bt, alive,
-    feat, cot, wa, wb, nb, act, edge,
-    in_sem, halo_send, halo_recv,
-):
-    me = lax.axis_index("dom")
-    edge[...] = jnp.zeros(edge.shape, BF16)
-    barrier = pltpu.get_barrier_semaphore()
-    pl.semaphore_signal(barrier, inc=1, device_id={"dom": (me + 1) % count})
-    pl.semaphore_signal(barrier, inc=1, device_id={"dom": (me + count - 1) % count})
-    loads = [
-        pltpu.make_async_copy(source, target, in_sem.at[i])
-        for i, (source, target) in enumerate(
-            ((act_in, act), (feat_in, feat), (cot_in, cot), (nb_in, nb), (wa_in, wa), (wb_in, wb))
-        )
-    ]
-    for load in loads:
-        load.start()
-    pl.semaphore_wait(barrier, 2)
-    places = []
-    for field, values in ((FEAT, feat_in), (GOUT, cot_in)):
-        places.append((values.at[:, E - 1], edge.at[field, 0]))
-        places.append((values.at[:, 0], edge.at[field, 1]))
-    halo = halo_copies(places, halo_send, halo_recv, count, me)
-    halo_start(halo, count, me)
-    for load in loads[:4]:
-        load.wait()
-    keep = [jnp.where(act[b] > 0, 1.0, 0.0) for b in range(2)]
-    given[FEAT] = jnp.concatenate([feat[b].astype(F32) for b in range(2)], axis=1).astype(BF16)
-    given[GOUT] = jnp.concatenate(
-        [cot[b].astype(F32) * keep[b] for b in range(2)], axis=1
-    ).astype(BF16)
-    rows = lax.broadcasted_iota(jnp.int32, (128, 128), 0)
-    alive[...] = jnp.where((rows & 8) == 0, keep[0], keep[1])
-    build_selection(nb, sel, sel_edge)
-    for field in (FEAT, GOUT):
-        pad_inner(given[field], sel, padded, field)
-    for load in loads[4:]:
-        load.wait()
-    build_bands(wa, band_a, band_at)
-    build_bands(wb, band_b, band_bt)
-    halo_wait(halo, count, me)
-    for field in (FEAT, GOUT):
-        below, above = [
-            edge[field, side].astype(F32).reshape(16, 512).astype(BF16) for side in range(2)
-        ]
-        pad_edge(below, above, sel_edge, padded, field)
-
-
 def kernel(
     ny, nz, scale,
-    given, padded, sel, sel_edge, band_a, band_at, band_b, band_bt, alive,
+    feat_in, wa_in, wb_in, nb_in, act_in, cot_in,
     out, gfeat, full,
+    feat, cot, wa, wb, nb, act, edge, given,
+    sel, sel_edge, padded, band_a, band_at, band_b, band_bt,
     late, late_padded, sums, from_core, chip, from_plane, groups,
+    in_sem, first_send, first_recv,
     halo_send, halo_recv, core_send, core_recv, plane_send, plane_recv,
     group_send, group_recv, back_send, back_recv, last_send, last_recv, relay,
 ):
@@ -286,34 +257,104 @@
     def at_group(step):
         return device_at((y, (z + step * ZLOW) % nz))
 
-    near = sorted({1, nhigh - 1})
-    far = nhigh > 3
-    greeted = [device_at(ahead(i)) for i in order]
-    greeted += [device_at(behind(i)) for i in order if steps[i][1] == 3]
-    greeted += [at_group(step) for step in (near if far else range(1, nhigh))]
-    greeted += [(me + 1) % count, (me + count - 1) % count]
+    def at_row(step):
+        return device_at((y, (z + nz + step) % nz))
+
+    def at_column(step):
+        return device_at((y ^ step, z))
+
+    def tell(number, devices):
+        for device in devices:
+            pl.semaphore_signal(relay.at[number], inc=1, device_id={"dom": device})
+
+    def hear(number, devices):
+        if devices:
+            pl.semaphore_wait(relay.at[number], len(devices))
+
+    columns = [at_column(step) for step in range(1, ny)]
+    ones, twos, fours = [[at_row(step), at_row(-step)] for step in (1, 2, 4)]
+    greeted = [(me + 1) % count, (me + count - 1) % count] + ones + columns
+
+    edge[...] = jnp.zeros(edge.shape, BF16)
     late[:, 0] = jnp.zeros((2, 16, 512), BF16)
     late[:, 9] = jnp.zeros((2, 16, 512), BF16)
     barrier = pltpu.get_barrier_semaphore()
     for device in greeted:
         pl.semaphore_signal(barrier, inc=1, device_id={"dom": device})
-
-    chip[HALF:, :] = jnp.zeros((CH * plane - HALF, 128), BF16)
+    loads = [
+        pltpu.make_async_copy(source, target, in_sem.at[i])
+        for i, (source, target) in enumerate(
+            ((act_in, act), (feat_in, feat), (cot_in, cot), (nb_in, nb), (wa_in, wa), (wb_in, wb))
+        )
+    ]
+    for load in loads:
+        load.start()
+    pl.semaphore_wait(barrier, len(greeted))
+    places = []
+    for field, values in ((FEAT, feat_in), (GOUT, cot_in)):
+        places.append((values.at[:, E - 1], edge.at[field, 0]))
+        places.append((values.at[:, 0], edge.at[field, 1]))
+    first = halo_copies(places, first_send, first_recv, count, me)
+    halo_start(first, count, me)
+    tell(0, ones)
+    for load in loads[:4]:
+        load.wait()
+    keep = [jnp.where(act[b] > 0, 1.0, 0.0) for b in range(2)]
+    given[FEAT] = jnp.concatenate([feat[b].astype(F32) for b in range(2)], axis=1).astype(BF16)
+    given[GOUT] = jnp.concatenate(
+        [cot[b].astype(F32) * keep[b] for b in range(2)], axis=1
+    ).astype(BF16)
+    rows = lax.broadcasted_iota(jnp.int32, (128, 128), 0)
+    alive = jnp.where((rows & 8) == 0, keep[0], keep[1])
+    build_selection(nb, sel, sel_edge)
+    for field in (FEAT, GOUT):
+        for c in range(3):
+            padded[field, 160 * c : 160 * c + 16, :] = jnp.zeros((16, 640), BF16)
+            padded[field, 160 * c + 144 : 160 * c + 160, :] = jnp.zeros((16, 640), BF16)
+        pad_inner(given[field], sel, padded, field)
+    for load in loads[4:]:
+        load.wait()
+    build_bands(wa, band_a, band_at)
+    build_bands(wb, band_b, band_bt)
+    hear(0, ones)
+    tell(1, twos)
+    tell(2, columns)
+    hidden = [convolve(padded, FEAT, band_a, pair, False) for pair in range(4)]
+    grad = [convolve(padded, GOUT, band_bt, pair, True) for pair in range(4)]
+    halo_wait(first, count, me)
+    for field in (FEAT, GOUT):
+        below, above = [
+            edge[field, side].astype(F32).reshape(16, 512).astype(BF16) for side in range(2)
+        ]
+        pad_edge(below, above, sel_edge, padded, field)
+    hidden_edge = convolve_edge(padded, FEAT, band_a, False)
+    grad_edge = convolve_edge(padded, GOUT, band_bt, True)
     for pair in range(4):
         lanes = slice(128 * pair, 128 * pair + 128)
-        h = convolve(padded, FEAT, band_a, pair, False)
-        g = convolve(padded, GOUT, band_bt, pair, True)
+        some = slice(16 * pair, 16 * pair + 16)
+
+        def joined(value, sides):
+            return jnp.concatenate(
+                [value[:16] + sides[0][some], value[16:112], value[112:] + sides[1][some]], axis=0
+            )
+
+        h = joined(hidden[pair], hidden_edge)
+        g = joined(grad[pair], grad_edge)
         s = jax.nn.sigmoid(h)
-        middle = alive[...] * (h * s)
+        middle = alive * (h * s)
         ghid = g * (s * (1.0 + h * (1.0 - s)))
         late[MID, 1:9, :, lanes] = middle.astype(BF16).reshape(8, 16, 128)
         late[GHID, 1:9, :, lanes] = ghid.astype(BF16).reshape(8, 16, 128)
+    halo = halo_copies(
+        ((late.at[:, E], late.at[:, 0]), (late.at[:, 1], late.at[:, E + 1])),
+        halo_send, halo_recv, count, me,
+    )
+    halo_start(halo, count, me)
+    hear(1, twos)
+    tell(3, fours)
+    chip[HALF:, :] = jnp.zeros((CH * plane - HALF, 128), BF16)
     for i in range(5):
         filter_taps(4 * (1 - core) + i, late, padded, sums)
-    pl.semaphore_wait(barrier, len(greeted))
-    if far:
-        for step in near:
-            pl.semaphore_signal(relay, inc=1, device_id={"dom": at_group(step)})
 
     own = pl.multiple_of(core * HALF, 8)
     other = pl.multiple_of((1 - core) * HALF, 8)
@@ -325,11 +366,6 @@
         device_id={"dom": partner},
     )
     to_core.start()
-    halo = halo_copies(
-        ((late.at[:, E], late.at[:, 0]), (late.at[:, 1], late.at[:, E + 1])),
-        halo_send, halo_recv, count, me,
-    )
-    halo_start(halo, count, me)
     for i in range(4):
         filter_taps(5 * core + i, late, padded, sums)
     to_core.wait_recv()
@@ -346,6 +382,7 @@
             device_id={"dom": device_at(ahead(i))},
         )
 
+    hear(2, columns)
     for i in order:
 
         @pl.when(spot_at(ahead(i)) < live)
@@ -357,7 +394,7 @@
             lanes = slice(128 * pair, 128 * pair + 128)
             value = convolve(late_padded, field, band, pair, flipped)
             if flipped:
-                value = value * alive[...]
+                value = value * alive
             value = value.reshape(8, 16, 128) + given[base, :, :, lanes].astype(F32)
             for b in range(2):
                 target[b, :, :, lanes] = value[:, 8 * b : 8 * b + 8].astype(BF16)
@@ -398,8 +435,7 @@
             device_id={"dom": partner},
         )
 
-    if far:
-        pl.semaphore_wait(relay, len(near))
+    hear(3, fours)
 
     @pl.when(spot < live)
     def _():
@@ -482,30 +518,42 @@
     brick = jax.ShapeDtypeStruct(features.shape, BF16)
     whole = pltpu.VMEM(features.shape, BF16)
     taps = pltpu.VMEM(weight_first.shape, BF16)
-    prepared = pl.pallas_call(
-        functools.partial(prepare, count),
-        out_shape=(
-            jax.ShapeDtypeStruct((2, 8, 16, 512), BF16),
-            jax.ShapeDtypeStruct((2, 480, 640), BF16),
-            jax.ShapeDtypeStruct((3, 384, 128), BF16),
-            jax.ShapeDtypeStruct((3, 96, 32), BF16),
-            jax.ShapeDtypeStruct((9, 256, 128), BF16),
-            jax.ShapeDtypeStruct((9, 128, 256), BF16),
-            jax.ShapeDtypeStruct((9, 256, 128), BF16),
-            jax.ShapeDtypeStruct((9, 128, 256), BF16),
-            jax.ShapeDtypeStruct((128, 128), F32),
-        ),
+    out, gfeat, full = pl.pallas_call(
+        functools.partial(kernel, ny, nz, scale),
+        out_shape=(brick, brick, jax.ShapeDtypeStruct((NCORE, plane, CH, 128), BF16)),
         in_specs=[hbm] * 6,
-        out_specs=(vmem,) * 9,
+        out_specs=(vmem, vmem, vmem),
         scratch_shapes=[
             whole, whole, taps, taps,
             pltpu.SMEM(neighbours.shape, jnp.int32),
             pltpu.SMEM(active.shape, jnp.int32),
             pltpu.VMEM((2, 2, 2, E, 512), BF16),
+            pltpu.VMEM((2, 8, 16, 512), BF16),
+            pltpu.VMEM((3, 384, 128), BF16),
+            pltpu.VMEM((3, 96, 32), BF16),
+            pltpu.VMEM((2, 480, 640), BF16),
+            pltpu.VMEM((9, 256, 128), BF16),
+            pltpu.VMEM((9, 128, 256), BF16),
+            pltpu.VMEM((9, 256, 128), BF16),
+            pltpu.VMEM((9, 128, 256), BF16),
+            pltpu.VMEM((2, 10, 16, 512), BF16),
+            pltpu.VMEM((2, 480, 640), BF16),
+            pltpu.VMEM((ROWS, 128), F32),
+            pltpu.VMEM((HALF, 128), F32),
+            pltpu.VMEM((plane * CH, 128), BF16),
+            pltpu.VMEM((plane - 1, CH, 128), BF16),
+            pltpu.VMEM((nhigh, CH, 128), BF16),
             dma((6,)), dma((4,)), dma((4,)),
+            dma((2,)), dma((2,)),
+            dma, dma,
+            dma((plane - 1,)), dma((plane - 1,)),
+            dma((nhigh - 1,)), dma((nhigh - 1,)),
+            dma((plane - 1,)), dma((plane - 1,)),
+            dma((plane,)), dma((plane,)),
+            pltpu.SemaphoreType.REGULAR((4,)),
         ],
         compiler_params=pltpu.CompilerParams(
-            collective_id=0, has_side_effects=True, vmem_limit_bytes=24 * 2**20
+            collective_id=0, has_side_effects=True, vmem_limit_bytes=40 * 2**20
         ),
     )(
         *[
@@ -515,31 +563,6 @@
             )
         ]
     )
-    out, gfeat, full = pl.pallas_call(
-        functools.partial(kernel, ny, nz, scale),
-        out_shape=(brick, brick, jax.ShapeDtypeStruct((NCORE, plane, CH, 128), BF16)),
-        in_specs=[vmem] * 9,
-        out_specs=(vmem, vmem, vmem),
-        scratch_shapes=[
-            pltpu.VMEM((2, 10, 16, 512), BF16),
-            pltpu.VMEM((2, 480, 640), BF16),
-            pltpu.VMEM((ROWS, 128), F32),
-            pltpu.VMEM((HALF, 128), F32),
-            pltpu.VMEM((plane * CH, 128), BF16),
-            pltpu.VMEM((plane - 1, CH, 128), BF16),
-            pltpu.VMEM((nhigh, CH, 128), BF16),
-            dma((2,)), dma((2,)),
-            dma, dma,
-            dma((plane - 1,)), dma((plane - 1,)),
-            dma((nhigh - 1,)), dma((nhigh - 1,)),
-            dma((plane - 1,)), dma((plane - 1,)),
-            dma((plane,)), dma((plane,)),
-            pltpu.SemaphoreType.REGULAR,
-        ],
-        compiler_params=pltpu.CompilerParams(
-            collective_id=1, has_side_effects=True, vmem_limit_bytes=24 * 2**20
-        ),
-    )(*prepared)
     grads = jax.ShapeDtypeStruct((ROWS, C), F32)
     out, gfeat, fa, fb = pl.pallas_call(
         finish,

time: 43.9 us -> 42.6 us (0.970)
  Pallas kernels: 43.1 us -> 41.8 us
    pallas_call x1 -> x0, Pallas kernels: 14.9 us -> none  [on_device(): pl.pallas_call(functools.partial(prepare, count), out_shape=(jax.ShapeDty...]
    pallas_call x1, Pallas kernels: 26.8 us -> 40.5 us  [on_device(): pl.pallas_call(functools.partial(kernel, ny, nz, scale), out_shape=(brick...]
where the time goes in v5:
time: 42.6 us; the launch traced here: 42.5 us
  Pallas kernels  41.8 us (98%)
  between operations  0.64 us (2%)
    pallas_call x1, Pallas kernels, on_device(): pl.pallas_call(functools.partial(kernel, ny, nz, scale), out_shape=(brick...  40.5 us
    pallas_call x1, Pallas kernels, on_device(): pl.pallas_call(finish, out_shape=(brick, brick, grads, grads), in_specs=[...  1.34 us

profile of v5, /device:TPU:1, one launch (start us, length us, event | category | flops | bytes accessed | tf_op | source)
XLA Modules:
  0.0 42.5 jit_solution(9702104038001680141)
XLA Ops:
  0.6 40.5 %shard_map.93 = (bf16[2,8,8,512]{3,2,1,0:T(8,128)(2,1)S(1)}, bf16[2,8,8,512]{3,2,1,0:T(8,128)(2,1)S(1)}, bf16[2,16,64,128]{3,2,1,0:T(8,128)(2,1)S(1)}) custom-call(bf16[2,8,8,512]{3,2,1,0:T(8,128)(2,1)} %feat_in.1, bf16[3,3,3,64,64]{4,3,2,1,0:T(8,128)(2,1)} %wa_in.1, bf16[3,3,3,64,64]{4,3,2,1,0:T(8,128)(2,1)} %wb_in.1, s32[2,26]{1,0:T(2,128)} %nb_in.1, ...), custom_call_target="tpu_custom_call" | custom-call | tf_op jit(solution)/shard_map/pallas_call | solution.py:521
  41.1 1.3 %shard_map.94 = (bf16[2,8,8,512]{3,2,1,0:T(8,128)(2,1)}, bf16[2,8,8,512]{3,2,1,0:T(8,128)(2,1)}, f32[1728,64]{1,0:T(8,128)}, f32[1728,64]{1,0:T(8,128)}) custom-call(bf16[2,8,8,512]{3,2,1,0:T(8,128)(2,1)S(1)} %get-tuple-element.11.out_in, bf16[2,8,8,512]{3,2,1,0:T(8,128)(2,1)S(1)} %get-tuple-element.12.gfeat_in, ...), custom_call_target="tpu_custom_call" | custom-call | tf_op jit(solution)/shard_map/pallas_call | solution.py:567

commit v6 on v5

--- a/solution.py
+++ b/solution.py
@@ -61,7 +61,7 @@
                     sel_edge[iz, 32 * c + 16 * side : 32 * c + 16 * side + 16, :] = hit[:, :32]
 
 
-def build_bands(weight, band, band_t):
+def build_band(weight, band):
     zero = jnp.zeros((C, C), BF16)
     for t in range(9):
         taps = [weight[t // 3, t % 3, e] for e in range(3)]
@@ -69,6 +69,12 @@
             left = taps[zi] if zi < 3 else zero
             right = taps[zi - 1] if zi > 0 else zero
             band[t, C * zi : C * zi + C, :] = jnp.concatenate([left, right], axis=1)
+
+
+def build_flipped(weight, band_t):
+    zero = jnp.zeros((C, C), BF16)
+    for t in range(9):
+        taps = [weight[t // 3, t % 3, e] for e in range(3)]
         band_t[8 - t, :C, :] = jnp.concatenate([taps[2], taps[1], taps[0], zero], axis=1)
         band_t[8 - t, C:, :] = jnp.concatenate([zero, taps[2], taps[1], taps[0]], axis=1)
 
@@ -289,14 +295,6 @@
     ]
     for load in loads:
         load.start()
-    pl.semaphore_wait(barrier, len(greeted))
-    places = []
-    for field, values in ((FEAT, feat_in), (GOUT, cot_in)):
-        places.append((values.at[:, E - 1], edge.at[field, 0]))
-        places.append((values.at[:, 0], edge.at[field, 1]))
-    first = halo_copies(places, first_send, first_recv, count, me)
-    halo_start(first, count, me)
-    tell(0, ones)
     for load in loads[:4]:
         load.wait()
     keep = [jnp.where(act[b] > 0, 1.0, 0.0) for b in range(2)]
@@ -307,6 +305,14 @@
     rows = lax.broadcasted_iota(jnp.int32, (128, 128), 0)
     alive = jnp.where((rows & 8) == 0, keep[0], keep[1])
     build_selection(nb, sel, sel_edge)
+    pl.semaphore_wait(barrier, len(greeted))
+    places = []
+    for field, values in ((FEAT, feat_in), (GOUT, cot_in)):
+        places.append((values.at[:, E - 1], edge.at[field, 0]))
+        places.append((values.at[:, 0], edge.at[field, 1]))
+    first = halo_copies(places, first_send, first_recv, count, me)
+    halo_start(first, count, me)
+    tell(0, ones)
     for field in (FEAT, GOUT):
         for c in range(3):
             padded[field, 160 * c : 160 * c + 16, :] = jnp.zeros((16, 640), BF16)
@@ -314,8 +320,8 @@
         pad_inner(given[field], sel, padded, field)
     for load in loads[4:]:
         load.wait()
-    build_bands(wa, band_a, band_at)
-    build_bands(wb, band_b, band_bt)
+    build_band(wa, band_a)
+    build_flipped(wb, band_bt)
     hear(0, ones)
     tell(1, twos)
     tell(2, columns)
@@ -369,8 +375,7 @@
     for i in range(4):
         filter_taps(5 * core + i, late, padded, sums)
     to_core.wait_recv()
-    from_core[...] = from_core[...] + sums[pl.ds(own, HALF), :]
-    chip[:HALF, :] = from_core[...].astype(BF16)
+    chip[:HALF, :] = (from_core[...] + sums[pl.ds(own, HALF), :]).astype(BF16)
 
     def plane_copy(i):
         begin = pl.multiple_of(spot_at(ahead(i)) * CH, CH)
@@ -399,6 +404,8 @@
             for b in range(2):
                 target[b, :, :, lanes] = value[:, 8 * b : 8 * b + 8].astype(BF16)
 
+    build_band(wb, band_b)
+    build_flipped(wa, band_at)
     halo_wait(halo, count, me)
     for field in (MID, GHID):
         pad_inner(late[field, 1:9], sel, late_padded, field)

time: 42.6 us -> 42.6 us (level)
  no operation moved by 1% of the time
where the time goes in v6:
time: 42.6 us; the launch traced here: 42.5 us
  Pallas kernels  41.8 us (98%)
  between operations  0.64 us (2%)
    pallas_call x1, Pallas kernels, on_device(): pl.pallas_call(functools.partial(kernel, ny, nz, scale), out_shape=(brick...  40.5 us
    pallas_call x1, Pallas kernels, on_device(): pl.pallas_call(finish, out_shape=(brick, brick, grads, grads), in_specs=[...  1.34 us

profile of v6, /device:TPU:1, one launch (start us, length us, event | category | flops | bytes accessed | tf_op | source)
XLA Modules:
  0.0 42.5 jit_solution(12853691821999780881)
XLA Ops:
  0.6 40.5 %shard_map.93 = (bf16[2,8,8,512]{3,2,1,0:T(8,128)(2,1)S(1)}, bf16[2,8,8,512]{3,2,1,0:T(8,128)(2,1)S(1)}, bf16[2,16,64,128]{3,2,1,0:T(8,128)(2,1)S(1)}) custom-call(bf16[2,8,8,512]{3,2,1,0:T(8,128)(2,1)} %feat_in.1, bf16[3,3,3,64,64]{4,3,2,1,0:T(8,128)(2,1)} %wa_in.1, bf16[3,3,3,64,64]{4,3,2,1,0:T(8,128)(2,1)} %wb_in.1, s32[2,26]{1,0:T(2,128)} %nb_in.1, ...), custom_call_target="tpu_custom_call" | custom-call | tf_op jit(solution)/shard_map/pallas_call | solution.py:528
  41.1 1.3 %shard_map.94 = (bf16[2,8,8,512]{3,2,1,0:T(8,128)(2,1)}, bf16[2,8,8,512]{3,2,1,0:T(8,128)(2,1)}, f32[1728,64]{1,0:T(8,128)}, f32[1728,64]{1,0:T(8,128)}) custom-call(bf16[2,8,8,512]{3,2,1,0:T(8,128)(2,1)S(1)} %get-tuple-element.11.out_in, bf16[2,8,8,512]{3,2,1,0:T(8,128)(2,1)S(1)} %get-tuple-element.12.gfeat_in, ...), custom_call_target="tpu_custom_call" | custom-call | tf_op jit(solution)/shard_map/pallas_call | solution.py:574
